TPU v7x, 512 devices: a whole 4x8x8 slice. The times are simulated.
512 devices in a mesh: seg: 32 (over x, y_lo, core), video: 16 (over y_hi, z).
Axes of the slice: x: 4, y: 8 (y_hi: 2, y_lo: 4; y = y_hi * 4 + y_lo), z: 8, core: 2. Of those that a mesh axis runs over, the one named last changes fastest.
Arguments:
- tokens: bfloat16 [2, 2048, 3072], P(None, 'seg'), may hold values from -6 to 6
- prompt_ids: int32 [2, 32], P(None, 'seg'), may hold values from 0 to 15
- prompt_table: bfloat16 [16, 3072], replicated, may hold values from -6 to 6
- qkv_weight: bfloat16 [3072, 3, 2048], P('seg', None, 'video'), may hold values from -0.109375 to 0.109375
- out_weight: bfloat16 [2048, 3072], P('seg', 'video'), may hold values from -0.125 to 0.125
- init_first: bfloat16 [32, 64, 256], P('video'), may hold values from -0.75 to 0.75
- init_second: bfloat16 [32, 64, 256], P('video'), may hold values from -0.375 to 0.375
- inner_rate: float32 [32], P('video'), may hold values from 0.002 to 0.02
Outputs:
- mixed: bfloat16 [2, 2048, 3072], P(None, 'seg', 'video')
All inputs are finite; a program needn't handle non-finite values.
Results may differ from a plain program's by a relative error of at most 0.01.
Values may be sent and summed in bfloat16 or wider, within the bound.
A program may use at most 64 MiB of HBM per device.

v0:
```python
import jax
import jax.numpy as jnp
from jax import lax
from jax.sharding import PartitionSpec as P

HS = 64


HIGH = lax.Precision.HIGHEST


def shifted(block, axis, distance):
    devices = range(lax.axis_size(axis))
    route = [(i - distance, i) for i in devices if i - distance in devices]
    return lax.ppermute(block, axis, route)


def inner_apply(first_layer, second_layer, inputs):
    pre_act = jnp.einsum("ms,si->mi", inputs, first_layer, precision=HIGH)
    hidden = jax.nn.gelu(pre_act, approximate=True)
    result = jnp.einsum("mi,si->ms", hidden, second_layer, precision=HIGH)
    centred = result - jnp.mean(result, -1, keepdims=True)
    spread = jnp.mean(centred * centred, -1, keepdims=True)
    return centred * lax.rsqrt(spread + 1e-06)


def inner_loss(first_layer, second_layer, keys_block, values_block):
    differ = inner_apply(first_layer, second_layer, keys_block) - (values_block - keys_block)
    return 0.5 * jnp.sum(differ * differ) / keys_block.shape[0]


def inner_step(first_layer, second_layer, rate, query_block, keys_block, values_block):
    grad_first, grad_second = jax.grad(inner_loss, argnums=(0, 1))(
        first_layer, second_layer, keys_block, values_block
    )
    first_layer = first_layer - rate * grad_first
    second_layer = second_layer - rate * grad_second
    return (
        first_layer,
        second_layer,
        query_block + inner_apply(first_layer, second_layer, query_block),
    )


def run_segment(state, rate, selected, visit_order):
    tok_rows, _, columns = selected.shape
    heads_local = columns // HS
    mini_rows = tok_rows // 4
    split = selected.astype(jnp.float32).reshape(4, mini_rows, 3, heads_local, HS)
    split = jnp.transpose(split, (2, 3, 0, 1, 4))
    layer_one = state[0]
    layer_two = state[1]
    results = [None, None, None, None]
    for minibatch in visit_order:
        layer_one, layer_two, answer = jax.vmap(inner_step)(
            layer_one,
            layer_two,
            rate,
            split[0, :, minibatch],
            split[1, :, minibatch],
            split[2, :, minibatch],
        )
        results[minibatch] = answer
    stacked = jnp.stack(results, axis=1)
    stacked = jnp.transpose(stacked, (1, 2, 0, 3)).reshape(tok_rows, columns)
    return (stacked, jnp.stack([layer_one, layer_two]).astype(jnp.bfloat16))


def advance(turn_index, answers, arrived, position, visit_order, starting, qkv, rate, initial):
    videos = qkv.shape[0]
    item = turn_index - position
    active = jnp.logical_and(item >= 0, item < videos)
    slot = jnp.clip(item, 0, videos - 1)
    state = jnp.where(starting, initial, arrived).astype(jnp.float32)

    def working(unused):
        selected = lax.dynamic_index_in_dim(qkv, slot, 0, keepdims=False)
        stacked, leaving = run_segment(state, rate, selected, visit_order)
        return (lax.dynamic_update_index_in_dim(answers, stacked, slot, 0), leaving)

    def resting(unused):
        return (answers, arrived)

    return lax.cond(active, working, resting, None)


def per_device(
    tokens, prompt_ids, prompt_table, qkv_weight, out_weight, init_first, init_second, inner_rate
):
    videos, tok_rows, width = tokens.shape
    prompts = prompt_table.shape[0]
    onehot = (prompt_ids[:, :, None] == jnp.arange(prompts, dtype=jnp.int32)).astype(jnp.float32)
    prompt_bias = jnp.einsum("vsp,pd->vsd", onehot, prompt_table.astype(jnp.float32))
    xin = (
        (tokens.astype(jnp.float32) + prompt_bias)
        .astype(jnp.bfloat16)
        .reshape(videos * tok_rows, width)
    )
    columns = qkv_weight.shape[2]
    picked = xin
    qkv = jnp.einsum(
        "td,dcj->tcj",
        picked,
        lax.all_gather(qkv_weight, "seg", axis=0, tiled=True),
        preferred_element_type=jnp.float32,
    )
    qkv = qkv.astype(jnp.bfloat16).reshape(videos, tok_rows, 3, columns)
    segments = lax.axis_size("seg")
    seg_index = lax.axis_index("seg")
    initial = jnp.stack([init_first, init_second])
    empty_state = jnp.zeros_like(initial)
    empty_answers = jnp.zeros((videos, tok_rows, columns), jnp.float32)
    turns = segments + videos - 1
    backward_pos = segments - 1 - seg_index
    onward_order = (0, 1, 2, 3)
    backward_order = (3, 2, 1, 0)

    def onward_turn(turn_index, carry):
        answers, arrived = carry
        answers, leaving = advance(
            turn_index,
            answers,
            arrived,
            seg_index,
            onward_order,
            seg_index == 0,
            qkv,
            inner_rate,
            initial,
        )
        arrived = shifted(leaving, "seg", 1)
        return (answers, arrived)

    def backward_turn(turn_index, carry):
        answers, arrived = carry
        answers, leaving = advance(
            turn_index,
            answers,
            arrived,
            backward_pos,
            backward_order,
            seg_index == segments - 1,
            qkv,
            inner_rate,
            initial,
        )
        arrived = shifted(leaving, "seg", -1)
        return (answers, arrived)

    onward_answers, _ = lax.fori_loop(0, turns, onward_turn, (empty_answers, empty_state))
    backward_answers, _ = lax.fori_loop(0, turns, backward_turn, (empty_answers, empty_state))
    heads = (onward_answers + backward_answers).astype(jnp.bfloat16)
    all_heads = lax.all_gather(heads, "video", axis=2, tiled=True).reshape(videos * tok_rows, -1)
    picked = all_heads
    mixed = jnp.dot(
        picked,
        lax.all_gather(out_weight, "seg", axis=0, tiled=True),
        preferred_element_type=jnp.float32,
    )
    return mixed.astype(jnp.bfloat16).reshape(videos, tok_rows, out_weight.shape[1])


def solution(mesh):
    return jax.shard_map(
        per_device,
        mesh=mesh,
        in_specs=(
            P(None, "seg", None),
            P(None, "seg"),
            P(),
            P("seg", None, "video"),
            P("seg", "video"),
            P("video", None, None),
            P("video", None, None),
            P("video"),
        ),
        out_specs=P(None, "seg", "video"),
        check_vma=False,
    )
```

profile of v0, /device:TPU:30, one launch (start us, length us, event | category | flops | bytes accessed | tf_op | source)
XLA Modules:
  0.0 1159.4 jit_solution(15012212535427147353)
XLA Ops:
  9.0 45.0 %all_gather.11 = bf16[2048,192]{1,0:T(8,128)(2,1)S(1)} all-gather(bf16[64,192]{1,0:T(8,128)(2,1)} %param.20), channel_id=1, replica_groups=mesh['seg'=32,'video'=16] {'seg'}, dimensions={0}, use_global_device_ids=true | all-gather | bytes 811008 | tf_op jit(solution)/shard_map/all_gather | solution.py:157
  55.4 19.6 %all-gather.2.cloned.1.call-done = bf16[3072,3,128]{2,0,1:T(8,128)(2,1)} async-done(((bf16[96,3,128]{2,0,1:T(8,128)(2,1)}), bf16[3072,3,128]{2,0,1:T(8,128)(2,1)}) %all-gather.2.cloned.1.call-update) | async-done | bytes 2359312 | tf_op jit(solution)/shard_map/all_gather | solution.py:104
  77.3 354.4 %while.34 = (s32[]{:T(128)}, f32[2,64,128]{2,1,0:T(8,128)S(1)}, bf16[2,2,64,256]{3,2,1,0:T(8,128)(2,1)S(1)}, s32[]{:T(128)}, pred[]{:T(512)}, /*index=5*/bf16[2,...) while((s32[]{:T(128)}, f32[2,64,128]{2,1,0:T(8,128)S(1)}, ...), condition=%wide.region_55.56_spmd, body=%wide.region_28.55_spmd.sunk | while | flops 178660480 | bytes 9039052 | solution.py:151
  80.0 10.6 collective-permute-done.1
  90.7 11.0 conditional.5
  106.2 11.0 conditional.5
  123.5 14.7 %collective-permute-start.1 = (bf16[2,2,64,256]{3,2,1,0:T(8,128)(2,1)S(1)}, bf16[2,2,64,256]{3,2,1,0:T(8,128)(2,1)S(1)}, u32[]{:S(2)}, u32[]{:S(2)}) collective-permute-start(bf16[2,2,64,256]{3,2,1,0:T(8,128)(2,1)S(1)} %get-tuple-element.667), channel_id=1, source_target_pairs={{16,0},{32,16},{48,32},{64,48},{80,64},{96,80},{112,96},{128,112},... | collective-permute-start | bytes 393224 | tf_op jit(solution)/shard_map/while/body/eval_jaxpr/ppermute | solution.py:15
  164.5 12.9 %collective-permute-start.1 = (bf16[2,2,64,256]{3,2,1,0:T(8,128)(2,1)S(1)}, bf16[2,2,64,256]{3,2,1,0:T(8,128)(2,1)S(1)}, u32[]{:S(2)}, u32[]{:S(2)}) collective-permute-start(bf16[2,2,64,256]{3,2,1,0:T(8,128)(2,1)S(1)} %get-tuple-element.667), channel_id=1, source_target_pairs={{16,0},{32,16},{48,32},{64,48},{80,64},{96,80},{112,96},{128,112},... | collective-permute-start | bytes 393224 | tf_op jit(solution)/shard_map/while/body/eval_jaxpr/ppermute | solution.py:15
  203.6 12.9 %collective-permute-start.1 = (bf16[2,2,64,256]{3,2,1,0:T(8,128)(2,1)S(1)}, bf16[2,2,64,256]{3,2,1,0:T(8,128)(2,1)S(1)}, u32[]{:S(2)}, u32[]{:S(2)}) collective-permute-start(bf16[2,2,64,256]{3,2,1,0:T(8,128)(2,1)S(1)} %get-tuple-element.667), channel_id=1, source_target_pairs={{16,0},{32,16},{48,32},{64,48},{80,64},{96,80},{112,96},{128,112},... | collective-permute-start | bytes 393224 | tf_op jit(solution)/shard_map/while/body/eval_jaxpr/ppermute | solution.py:15
  243.6 17.4 %collective-permute-start.1 = (bf16[2,2,64,256]{3,2,1,0:T(8,128)(2,1)S(1)}, bf16[2,2,64,256]{3,2,1,0:T(8,128)(2,1)S(1)}, u32[]{:S(2)}, u32[]{:S(2)}) collective-permute-start(bf16[2,2,64,256]{3,2,1,0:T(8,128)(2,1)S(1)} %get-tuple-element.667), channel_id=1, source_target_pairs={{16,0},{32,16},{48,32},{64,48},{80,64},{96,80},{112,96},{128,112},... | collective-permute-start | bytes 393224 | tf_op jit(solution)/shard_map/while/body/eval_jaxpr/ppermute | solution.py:15
  408.2 12.0 %collective-permute-start.1 = (bf16[2,2,64,256]{3,2,1,0:T(8,128)(2,1)S(1)}, bf16[2,2,64,256]{3,2,1,0:T(8,128)(2,1)S(1)}, u32[]{:S(2)}, u32[]{:S(2)}) collective-permute-start(bf16[2,2,64,256]{3,2,1,0:T(8,128)(2,1)S(1)} %get-tuple-element.667), channel_id=1, source_target_pairs={{16,0},{32,16},{48,32},{64,48},{80,64},{96,80},{112,96},{128,112},... | collective-permute-start | bytes 393224 | tf_op jit(solution)/shard_map/while/body/eval_jaxpr/ppermute | solution.py:15
  431.8 663.1 %while.33 = (s32[]{:T(128)}, f32[2,64,128]{2,1,0:T(8,128)S(1)}, bf16[2,2,64,256]{3,2,1,0:T(8,128)(2,1)S(1)}, s32[]{:T(128)}, pred[]{:T(512)}, /*index=5*/bf16[2,...) while((s32[]{:T(128)}, f32[2,64,128]{2,1,0:T(8,128)S(1)}, ...), condition=%wide.region_27.28_spmd, body=%wide.region_0.27_spmd.sunk | while | flops 178660480 | bytes 9039052 | solution.py:150
  451.9 10.0 collective-permute-done
  491.0 10.0 collective-permute-done
  530.3 9.8 collective-permute-done
  569.4 12.5 %collective-permute-done = bf16[2,2,64,256]{3,2,1,0:T(8,128)(2,1)S(1)} collective-permute-done((bf16[2,2,64,256]{3,2,1,0:T(8,128)(2,1)S(1)}, bf16[2,2,64,256]{3,2,1,0:T(8,128)(2,1)S(1)}, u32[]{:S(2)}, u32[]{:S(2)}) %collective-permute-start) | collective-permute-done | bytes 131104 | tf_op jit(solution)/shard_map/while/body/eval_jaxpr/ppermute | solution.py:15
  611.2 9.8 collective-permute-done
  650.3 10.4 collective-permute-done
  690.0 9.3 collective-permute-done
  719.5 327.3 %collective-permute-done = bf16[2,2,64,256]{3,2,1,0:T(8,128)(2,1)S(1)} collective-permute-done((bf16[2,2,64,256]{3,2,1,0:T(8,128)(2,1)S(1)}, bf16[2,2,64,256]{3,2,1,0:T(8,128)(2,1)S(1)}, u32[]{:S(2)}, u32[]{:S(2)}) %collective-permute-start) | collective-permute-done | bytes 131104 | tf_op jit(solution)/shard_map/while/body/eval_jaxpr/ppermute | solution.py:15
  1046.8 10.9 conditional.4
  1066.8 10.9 conditional.4
  1084.1 9.8 collective-permute-start
  1094.9 56.4 %all_gather.10 = bf16[2,64,2048]{2,1,0:T(8,128)(2,1)S(1)} all-gather(bf16[2,64,128]{2,1,0:T(8,128)(2,1)S(1)} %add_convert_fusion.1), channel_id=1, replica_groups=mesh['seg'=32,'video'=16] {'video'}, dimensions={2}, use_global_device_ids=true | all-gather | bytes 557056 | tf_op jit(solution)/shard_map/all_gather | solution.py:153
  (635 shorter events, 531.0 us)
Async XLA Ops:
  6.5 68.4 %all-gather.2.cloned.1.call-start = ((), (), s32[]{:S(2)}) async-start(), calls=%async_computation | async-start | bytes 2433024 | tf_op jit(solution)/shard_map/all_gather | solution.py:104
  77.4 13.3 %collective-permute-start.1 = (bf16[2,2,64,256]{3,2,1,0:T(8,128)(2,1)S(1)}, bf16[2,2,64,256]{3,2,1,0:T(8,128)(2,1)S(1)}, u32[]{:S(2)}, u32[]{:S(2)}) collective-permute-start(bf16[2,2,64,256]{3,2,1,0:T(8,128)(2,1)S(1)} %get-tuple-element.667), channel_id=1, source_target_pairs={{16,0},{32,16},{48,32},{64,48},{80,64},{96,80},{112,96},{128,112},... | collective-permute-start | bytes 393224 | tf_op jit(solution)/shard_map/while/body/eval_jaxpr/ppermute | solution.py:15
  123.5 17.2 %collective-permute-start.1 = (bf16[2,2,64,256]{3,2,1,0:T(8,128)(2,1)S(1)}, bf16[2,2,64,256]{3,2,1,0:T(8,128)(2,1)S(1)}, u32[]{:S(2)}, u32[]{:S(2)}) collective-permute-start(bf16[2,2,64,256]{3,2,1,0:T(8,128)(2,1)S(1)} %get-tuple-element.667), channel_id=1, source_target_pairs={{16,0},{32,16},{48,32},{64,48},{80,64},{96,80},{112,96},{128,112},... | collective-permute-start | bytes 393224 | tf_op jit(solution)/shard_map/while/body/eval_jaxpr/ppermute | solution.py:15
  147.2 10.8 collective-permute-start.1
  164.5 15.4 %collective-permute-start.1 = (bf16[2,2,64,256]{3,2,1,0:T(8,128)(2,1)S(1)}, bf16[2,2,64,256]{3,2,1,0:T(8,128)(2,1)S(1)}, u32[]{:S(2)}, u32[]{:S(2)}) collective-permute-start(bf16[2,2,64,256]{3,2,1,0:T(8,128)(2,1)S(1)} %get-tuple-element.667), channel_id=1, source_target_pairs={{16,0},{32,16},{48,32},{64,48},{80,64},{96,80},{112,96},{128,112},... | collective-permute-start | bytes 393224 | tf_op jit(solution)/shard_map/while/body/eval_jaxpr/ppermute | solution.py:15
  186.3 10.8 collective-permute-start.1
  203.6 15.4 %collective-permute-start.1 = (bf16[2,2,64,256]{3,2,1,0:T(8,128)(2,1)S(1)}, bf16[2,2,64,256]{3,2,1,0:T(8,128)(2,1)S(1)}, u32[]{:S(2)}, u32[]{:S(2)}) collective-permute-start(bf16[2,2,64,256]{3,2,1,0:T(8,128)(2,1)S(1)} %get-tuple-element.667), channel_id=1, source_target_pairs={{16,0},{32,16},{48,32},{64,48},{80,64},{96,80},{112,96},{128,112},... | collective-permute-start | bytes 393224 | tf_op jit(solution)/shard_map/while/body/eval_jaxpr/ppermute | solution.py:15
  225.4 10.8 collective-permute-start.1
  243.6 19.9 %collective-permute-start.1 = (bf16[2,2,64,256]{3,2,1,0:T(8,128)(2,1)S(1)}, bf16[2,2,64,256]{3,2,1,0:T(8,128)(2,1)S(1)}, u32[]{:S(2)}, u32[]{:S(2)}) collective-permute-start(bf16[2,2,64,256]{3,2,1,0:T(8,128)(2,1)S(1)} %get-tuple-element.667), channel_id=1, source_target_pairs={{16,0},{32,16},{48,32},{64,48},{80,64},{96,80},{112,96},{128,112},... | collective-permute-start | bytes 393224 | tf_op jit(solution)/shard_map/while/body/eval_jaxpr/ppermute | solution.py:15
  290.8 11.8 %collective-permute-start.1 = (bf16[2,2,64,256]{3,2,1,0:T(8,128)(2,1)S(1)}, bf16[2,2,64,256]{3,2,1,0:T(8,128)(2,1)S(1)}, u32[]{:S(2)}, u32[]{:S(2)}) collective-permute-start(bf16[2,2,64,256]{3,2,1,0:T(8,128)(2,1)S(1)} %get-tuple-element.667), channel_id=1, source_target_pairs={{16,0},{32,16},{48,32},{64,48},{80,64},{96,80},{112,96},{128,112},... | collective-permute-start | bytes 393224 | tf_op jit(solution)/shard_map/while/body/eval_jaxpr/ppermute | solution.py:15
  329.9 11.8 %collective-permute-start.1 = (bf16[2,2,64,256]{3,2,1,0:T(8,128)(2,1)S(1)}, bf16[2,2,64,256]{3,2,1,0:T(8,128)(2,1)S(1)}, u32[]{:S(2)}, u32[]{:S(2)}) collective-permute-start(bf16[2,2,64,256]{3,2,1,0:T(8,128)(2,1)S(1)} %get-tuple-element.667), channel_id=1, source_target_pairs={{16,0},{32,16},{48,32},{64,48},{80,64},{96,80},{112,96},{128,112},... | collective-permute-start | bytes 393224 | tf_op jit(solution)/shard_map/while/body/eval_jaxpr/ppermute | solution.py:15
  369.0 11.8 %collective-permute-start.1 = (bf16[2,2,64,256]{3,2,1,0:T(8,128)(2,1)S(1)}, bf16[2,2,64,256]{3,2,1,0:T(8,128)(2,1)S(1)}, u32[]{:S(2)}, u32[]{:S(2)}) collective-permute-start(bf16[2,2,64,256]{3,2,1,0:T(8,128)(2,1)S(1)} %get-tuple-element.667), channel_id=1, source_target_pairs={{16,0},{32,16},{48,32},{64,48},{80,64},{96,80},{112,96},{128,112},... | collective-permute-start | bytes 393224 | tf_op jit(solution)/shard_map/while/body/eval_jaxpr/ppermute | solution.py:15
  408.2 14.5 %collective-permute-start.1 = (bf16[2,2,64,256]{3,2,1,0:T(8,128)(2,1)S(1)}, bf16[2,2,64,256]{3,2,1,0:T(8,128)(2,1)S(1)}, u32[]{:S(2)}, u32[]{:S(2)}) collective-permute-start(bf16[2,2,64,256]{3,2,1,0:T(8,128)(2,1)S(1)} %get-tuple-element.667), channel_id=1, source_target_pairs={{16,0},{32,16},{48,32},{64,48},{80,64},{96,80},{112,96},{128,112},... | collective-permute-start | bytes 393224 | tf_op jit(solution)/shard_map/while/body/eval_jaxpr/ppermute | solution.py:15
  431.8 9.1 collective-permute-start
  450.0 11.9 %collective-permute-start = (bf16[2,2,64,256]{3,2,1,0:T(8,128)(2,1)S(1)}, bf16[2,2,64,256]{3,2,1,0:T(8,128)(2,1)S(1)}, u32[]{:S(2)}, u32[]{:S(2)}) collective-permute-start(bf16[2,2,64,256]{3,2,1,0:T(8,128)(2,1)S(1)} %get-tuple-element.657), channel_id=1, source_target_pairs={{0,16},{16,32},{32,48},{48,64},{64,80},{80,96},{96,112},{112,128},... | collective-permute-start | bytes 393224 | tf_op jit(solution)/shard_map/while/body/eval_jaxpr/ppermute | solution.py:15
  471.0 9.1 collective-permute-start
  489.1 11.9 %collective-permute-start = (bf16[2,2,64,256]{3,2,1,0:T(8,128)(2,1)S(1)}, bf16[2,2,64,256]{3,2,1,0:T(8,128)(2,1)S(1)}, u32[]{:S(2)}, u32[]{:S(2)}) collective-permute-start(bf16[2,2,64,256]{3,2,1,0:T(8,128)(2,1)S(1)} %get-tuple-element.657), channel_id=1, source_target_pairs={{0,16},{16,32},{32,48},{48,64},{64,80},{80,96},{96,112},{112,128},... | collective-permute-start | bytes 393224 | tf_op jit(solution)/shard_map/while/body/eval_jaxpr/ppermute | solution.py:15
  528.4 11.8 %collective-permute-start = (bf16[2,2,64,256]{3,2,1,0:T(8,128)(2,1)S(1)}, bf16[2,2,64,256]{3,2,1,0:T(8,128)(2,1)S(1)}, u32[]{:S(2)}, u32[]{:S(2)}) collective-permute-start(bf16[2,2,64,256]{3,2,1,0:T(8,128)(2,1)S(1)} %get-tuple-element.657), channel_id=1, source_target_pairs={{0,16},{16,32},{32,48},{48,64},{64,80},{80,96},{96,112},{112,128},... | collective-permute-start | bytes 393224 | tf_op jit(solution)/shard_map/while/body/eval_jaxpr/ppermute | solution.py:15
  567.5 14.5 %collective-permute-start = (bf16[2,2,64,256]{3,2,1,0:T(8,128)(2,1)S(1)}, bf16[2,2,64,256]{3,2,1,0:T(8,128)(2,1)S(1)}, u32[]{:S(2)}, u32[]{:S(2)}) collective-permute-start(bf16[2,2,64,256]{3,2,1,0:T(8,128)(2,1)S(1)} %get-tuple-element.657), channel_id=1, source_target_pairs={{0,16},{16,32},{32,48},{48,64},{64,80},{80,96},{96,112},{112,128},... | collective-permute-start | bytes 393224 | tf_op jit(solution)/shard_map/while/body/eval_jaxpr/ppermute | solution.py:15
  609.3 11.8 %collective-permute-start = (bf16[2,2,64,256]{3,2,1,0:T(8,128)(2,1)S(1)}, bf16[2,2,64,256]{3,2,1,0:T(8,128)(2,1)S(1)}, u32[]{:S(2)}, u32[]{:S(2)}) collective-permute-start(bf16[2,2,64,256]{3,2,1,0:T(8,128)(2,1)S(1)} %get-tuple-element.657), channel_id=1, source_target_pairs={{0,16},{16,32},{32,48},{48,64},{64,80},{80,96},{96,112},{112,128},... | collective-permute-start | bytes 393224 | tf_op jit(solution)/shard_map/while/body/eval_jaxpr/ppermute | solution.py:15
  648.4 12.3 %collective-permute-start = (bf16[2,2,64,256]{3,2,1,0:T(8,128)(2,1)S(1)}, bf16[2,2,64,256]{3,2,1,0:T(8,128)(2,1)S(1)}, u32[]{:S(2)}, u32[]{:S(2)}) collective-permute-start(bf16[2,2,64,256]{3,2,1,0:T(8,128)(2,1)S(1)} %get-tuple-element.657), channel_id=1, source_target_pairs={{0,16},{16,32},{32,48},{48,64},{64,80},{80,96},{96,112},{112,128},... | collective-permute-start | bytes 393224 | tf_op jit(solution)/shard_map/while/body/eval_jaxpr/ppermute | solution.py:15
  688.0 11.2 collective-permute-start
  717.5 329.2 %collective-permute-start = (bf16[2,2,64,256]{3,2,1,0:T(8,128)(2,1)S(1)}, bf16[2,2,64,256]{3,2,1,0:T(8,128)(2,1)S(1)}, u32[]{:S(2)}, u32[]{:S(2)}) collective-permute-start(bf16[2,2,64,256]{3,2,1,0:T(8,128)(2,1)S(1)} %get-tuple-element.657), channel_id=1, source_target_pairs={{0,16},{16,32},{32,48},{48,64},{64,80},{80,96},{96,112},{112,128},... | collective-permute-start | bytes 393224 | tf_op jit(solution)/shard_map/while/body/eval_jaxpr/ppermute | solution.py:15
  1084.1 10.8 collective-permute-start
  (45 other events, 385.4 us)
Sparse Core Ops, SparseCore 0:
  9.5 65.4 all-gather.1
where the time goes:
time: 1160 us
  waiting for transfers between devices  678 us (58%)
  starting transfers between devices  310 us (27%)
  blocking collectives  101 us (9%)
  matrix products  33 us (3%)
  other arithmetic  16.3 us (1%)
  between operations  13.5 us (1%)
    ppermute x66, waiting for transfers between devices, shifted(): return lax.ppermute(block, axis, route)  657 us
    ppermute x66, starting transfers between devices, shifted(): return lax.ppermute(block, axis, route)  310 us
    all_gather x1, blocking collectives, per_device(): lax.all_gather(heads, 'video', axis=2, tiled=True)  56.4 us
    all_gather x1, blocking collectives, per_device(): lax.all_gather(out_weight, 'seg', axis=0, tiled=True)  45 us
  transfers between devices with their start and end apart: 67, of which 67 were waited for; matrix products, arithmetic and copies ran while one was open for 0% of the time, Pallas kernels for 0%

commit v1 on v0

v1 whole, which is shorter than its diff:
```python
import jax
import jax.numpy as jnp
from jax import lax
from jax.experimental import pallas as pl
from jax.experimental.pallas import tpu as pltpu
from jax.sharding import PartitionSpec as P

HS = 64
MINI = 16
SEGS = 32
GROUPS = 16
VIDEOS = 2
ROWS = 64
EPS = 1e-6
C0 = 0.7978845608028654
C1 = C0 * 0.044715
f32 = jnp.float32
bf16 = jnp.bfloat16


def contract(a, b, da, db):
    return lax.dot_general(a, b, (((da,), (db,)), ((), ())), preferred_element_type=f32)


def nn(a, b):
    return contract(a, b, 1, 0)


def nt(a, b):
    return contract(a, b, 1, 1)


def tn(a, b):
    return contract(a, b, 0, 0)


def gelu_parts(x):
    x2 = x * x
    t = jnp.tanh(x * (C0 + C1 * x2))
    half = 0.5 * x
    return half + half * t, t, x2, half


def gelu_slope(t, x2, half):
    return (0.5 + 0.5 * t) + half * (1.0 - t * t) * (C0 + (3.0 * C1) * x2)


def remote(src, dst, send, recv, seg=None, video=None):
    where = {"seg": seg} if video is None else {"video": video}
    return pltpu.make_async_remote_copy(
        src_ref=src,
        dst_ref=dst,
        send_sem=send,
        recv_sem=recv,
        device_id=where,
        device_id_type=pl.DeviceIdType.MESH,
    )


def landed(ref, sem):
    pltpu.make_async_copy(ref, ref, sem).wait()


def kernel(
    rate_ref,
    ids_ref,
    tok_ref,
    table_ref,
    w_ref,
    ow_ref,
    first_ref,
    second_ref,
    out_ref,
    tok,
    xin,
    wall,
    acc,
    qmsg,
    qin,
    zst,
    zbuf,
    owall,
    heads,
    first,
    second,
    load_sem,
    w_send,
    w_recv,
    y_send,
    q_send,
    q_recv,
    o_send,
    o_recv,
    z_send,
    z_recv,
    h_send,
    h_recv,
):
    me = lax.axis_index("seg")
    vid = lax.axis_index("video")
    core = me % 2
    chip = me // 2
    x = chip // 4
    y = chip % 4

    def at(xx, yy, cc):
        return ((xx % 4) * 4 + yy) * 2 + cc

    load = pltpu.make_async_copy(tok_ref, tok, load_sem)
    load.start()

    barrier = pltpu.get_barrier_semaphore()

    def greet_seg(i, carry):
        pl.semaphore_signal(
            barrier, inc=1, device_id={"seg": (me + i) % SEGS}, device_id_type=pl.DeviceIdType.MESH
        )
        return carry

    def greet_video(i, carry):
        pl.semaphore_signal(
            barrier, inc=1, device_id={"video": (vid + i) % GROUPS}, device_id_type=pl.DeviceIdType.MESH
        )
        return carry

    lax.fori_loop(1, SEGS, greet_seg, 0)
    lax.fori_loop(1, GROUPS, greet_video, 0)
    pl.semaphore_wait(barrier, SEGS - 1 + GROUPS - 1)

    right, left, mate = at(x + 1, y, core), at(x + 3, y, core), at(x, y, 1 - core)
    y1 = y + 1 - 2 * (y % 2)
    y2 = (y + 2) % 4
    y3 = 3 - y

    def y_of(k):
        return jnp.where(k == 0, y, jnp.where(k == 1, y1, jnp.where(k == 2, y2, y3)))

    def pass_on(chunk, which, target, src=None):
        remote(
            wall.at[chunk] if src is None else src,
            wall.at[chunk],
            w_send.at[chunk, which],
            w_recv.at[chunk],
            seg=target,
        ).start()

    for k, yy in enumerate((y1, y2, y3)):
        remote(w_ref, wall.at[me], y_send.at[k], w_recv.at[me], seg=at(x, yy, core)).start()
    pass_on(me, 0, right, w_ref)
    pass_on(me, 1, left, w_ref)
    pass_on(me, 2, mate, w_ref)
    wall[me] = w_ref[...]

    load.wait()
    lane = lax.broadcasted_iota(jnp.int32, (16, 16), 1)
    picks = [jnp.where(lane == ids_ref[v, 0], 1.0, 0.0).astype(bf16) for v in range(VIDEOS)]

    def prepare(g, carry):
        span = pl.ds(pl.multiple_of(g * 384, 128), 384)
        for v in range(VIDEOS):
            bias = nn(picks[v], table_ref[:, span])[0:1]
            part = (tok[v, :, span].astype(f32) + bias).astype(bf16)
            for i in range(4):
                xin[g * 4 + i, ROWS * v : ROWS * (v + 1), 0:96] = part[:, 96 * i : 96 * (i + 1)]
        return carry

    def y_step(k, carry):
        chunk = at(x, y_of(k), core)
        landed(wall.at[chunk], w_recv.at[chunk])
        pass_on(chunk, 0, right)
        pass_on(chunk, 1, left)
        pass_on(chunk, 2, mate)
        return carry

    def add(chunk):
        acc[...] += nn(xin[chunk, :, 0:96], wall[chunk])

    lax.fori_loop(0, 8, prepare, 0)
    lax.fori_loop(1, 4, y_step, 0)
    acc[...] = jnp.zeros_like(acc)

    def x_step(k, carry):
        row = y_of(k)
        a = at(x + 3, row, core)
        b = at(x + 1, row, core)
        landed(wall.at[a], w_recv.at[a])
        pass_on(a, 2, mate)

        @pl.when(row < 2)
        def _():
            pass_on(a, 0, right)

        landed(wall.at[b], w_recv.at[b])
        pass_on(b, 2, mate)

        @pl.when(row >= 2)
        def _():
            pass_on(b, 1, left)

        add(at(x, row, core))
        add(a)
        add(b)
        c = at(x, row, 1 - core)
        landed(wall.at[c], w_recv.at[c])
        add(c)
        return carry

    lax.fori_loop(0, 4, x_step, 0)

    def far_step(k, carry):
        row = y_of(k)
        a = at(x + 2, row, core)
        landed(wall.at[a], w_recv.at[a])
        pass_on(a, 2, mate)
        add(a)
        for i in (1, 3):
            c = at(x + i, row, 1 - core)
            landed(wall.at[c], w_recv.at[c])
            add(c)
        return carry

    lax.fori_loop(0, 4, far_step, 0)

    def last_step(k, carry):
        c = at(x + 2, y_of(k), 1 - core)
        landed(wall.at[c], w_recv.at[c])
        add(c)
        return carry

    lax.fori_loop(0, 4, last_step, 0)

    for j in range(3):
        part = acc[:, 128 * j : 128 * (j + 1)]
        turned = pltpu.roll(part, 64, 1)
        for v in range(VIDEOS):
            qmsg[2 * v, j] = part[ROWS * v : ROWS * (v + 1)].astype(bf16)
            qmsg[2 * v + 1, j] = turned[ROWS * v : ROWS * (v + 1)].astype(bf16)

    def owner_of(i):
        return jnp.where(i < 4, i, SEGS - 8 + i)

    def give(i, carry):
        owner = owner_of(i)

        @pl.when(owner == me)
        def _():
            pltpu.make_async_copy(qmsg.at[i % 4], qin.at[me], q_recv.at[me]).start()

        @pl.when(owner != me)
        def _():
            remote(qmsg.at[i % 4], qin.at[me], q_send.at[i], q_recv.at[me], seg=owner).start()

        return carry

    lax.fori_loop(0, 8, give, 0)

    def give_out_weight(i):
        target = (me + i) % SEGS
        here = pl.ds(pl.multiple_of(me * 64, 64), 64)
        remote(ow_ref, owall.at[here], o_send.at[i], o_recv.at[me], seg=target).start()

    owall[pl.ds(pl.multiple_of(me * 64, 64), 64)] = ow_ref[...]

    is_owner = jnp.logical_or(me < 4, me >= SEGS - 4)
    back = jnp.where(me < 4, 0, 1)
    slot = jnp.where(me < 4, me, me - (SEGS - 8))
    head = me % 2

    def seg_of(j):
        return j + back * (SEGS - 1 - 2 * j)

    def give_answers(j):
        target = seg_of(j)

        @pl.when(target == me)
        def _():
            pltpu.make_async_copy(zst.at[target], zbuf.at[slot], z_recv.at[slot]).start()

        @pl.when(target != me)
        def _():
            remote(zst.at[target], zbuf.at[slot], z_send.at[target], z_recv.at[slot], seg=target).start()

    @pl.when(is_owner)
    def _():
        eta = rate_ref[head]
        first[...] = first_ref[head]
        second[...] = second_ref[head]
        offs = [pl.multiple_of(MINI * (t + back * (3 - 2 * t)), MINI) for t in range(4)]

        def segment(j, qprev):
            s = seg_of(j)
            before = jnp.where(j == 0, SEGS, seg_of(j - 1))
            landed(qin.at[s], q_recv.at[s])
            qs = [qin[s, 0, pl.ds(offs[t], MINI), 0:HS] for t in range(4)]
            ks = [qin[s, 1, pl.ds(offs[t], MINI), 0:HS] for t in range(4)]
            vs = [qin[s, 2, pl.ds(offs[t], MINI), 0:HS] for t in range(4)]
            keys = jnp.concatenate(ks, 0)
            both = jnp.concatenate([qprev, ks[0], qs[0], ks[1], qs[1], ks[2], qs[2], ks[3]], 0)
            layer_one = first[...]
            layer_two = second[...].astype(f32)
            mu = jnp.mean(layer_two, 0, keepdims=True)
            centred = layer_two - mu
            pre_all = nn(both, layer_one)
            cross = (-eta * nt(both, keys)).astype(bf16)
            pres = [pre_all[32 * t : 32 * t + 32] for t in range(4)]
            grads = []
            for t in range(4):
                target = vs[t].astype(f32) - ks[t].astype(f32)
                target = target - jnp.mean(target, -1, keepdims=True)
                h, th, x2, half = gelu_parts(pres[t])
                hb = h.astype(bf16)
                weights = centred.astype(bf16)
                c = nt(hb, weights)
                w = nn(target.astype(bf16), weights)
                ck = c[MINI:]
                u = nn(ck.astype(bf16), weights)
                rho = lax.rsqrt(jnp.mean(c * c, -1, keepdims=True) + EPS)
                m = jnp.mean(target * ck, -1, keepdims=True)
                rk = rho[MINI:]
                r2 = rk * rk
                b = rk * (1.0 / MINI)
                a = (r2 * (1.0 / MINI)) * (EPS * r2 + rk * m)
                slope = gelu_slope(th[MINI:], x2[MINI:], half[MINI:])
                grad = ((a * u - b * w) * slope).astype(bf16)
                grads.append(grad)
                for r in range(t + 1, 4):
                    pres[r] = pres[r] + nn(cross[32 * r : 32 * r + 32, MINI * t : MINI * (t + 1)], grad)
                d = a * ck - b * target
                centred = centred - eta * tn(d.astype(bf16), hb[MINI:])
                qq = qprev if t == 0 else qs[t - 1]
                answer = qq.astype(f32) + c[:MINI] * rho[:MINI]
                if t == 0:
                    zst[before, pl.ds(offs[3], MINI), 0:HS] = answer
                else:
                    zst[s, pl.ds(offs[t - 1], MINI), 0:HS] = answer
            grad = jnp.concatenate(grads, 0)
            first[...] = (layer_one.astype(f32) - eta * tn(keys, grad)).astype(bf16)
            second[...] = (centred + mu).astype(bf16)

            @pl.when(j >= 1)
            def _():
                give_answers(j - 1)
                give_out_weight(j)

            return qs[3]

        qlast = lax.fori_loop(0, SEGS, segment, jnp.zeros((MINI, HS), bf16))
        layer_two = second[...].astype(f32)
        centred = (layer_two - jnp.mean(layer_two, 0, keepdims=True)).astype(bf16)
        h = gelu_parts(nn(qlast, first[...]))[0]
        c = nt(h.astype(bf16), centred)
        rho = lax.rsqrt(jnp.mean(c * c, -1, keepdims=True) + EPS)
        zst[seg_of(SEGS - 1), pl.ds(offs[3], MINI), 0:HS] = qlast.astype(f32) + c * rho
        give_answers(SEGS - 1)

    @pl.when(jnp.logical_not(is_owner))
    def _():
        def one(i, carry):
            give_out_weight(i)
            return carry

        lax.fori_loop(1, SEGS, one, 0)

    for i in range(8):
        landed(zbuf.at[i], z_recv.at[i])
    for v in range(VIDEOS):
        pair = [(zbuf[2 * v + h, :, 0:HS] + zbuf[4 + 2 * v + h, :, 0:HS]).astype(bf16) for h in range(2)]
        heads[vid, ROWS * v : ROWS * (v + 1)] = jnp.concatenate(pair, 1)

    def give_heads(i, carry):
        remote(heads.at[vid], heads.at[vid], h_send.at[i], h_recv.at[vid], video=(vid + i) % GROUPS).start()
        return carry

    lax.fori_loop(1, GROUPS, give_heads, 0)

    def out_weight_landed(i, carry):
        r = (me + i) % SEGS
        landed(owall.at[pl.ds(pl.multiple_of(r * 64, 64), 64)], o_recv.at[r])
        return carry

    lax.fori_loop(1, SEGS, out_weight_landed, 0)

    def project(i, total):
        g = (vid + i) % GROUPS

        @pl.when(i > 0)
        def _():
            landed(heads.at[g], h_recv.at[g])

        return total + nn(heads[g], owall[pl.ds(pl.multiple_of(g * 128, 128), 128)])

    total = lax.fori_loop(0, GROUPS, project, jnp.zeros((VIDEOS * ROWS, 192), f32))
    out_ref[...] = total.astype(bf16)

    for k in range(3):
        remote(w_ref, wall.at[me], y_send.at[k], w_recv.at[me], seg=right).wait_send()

    def sent(chunk, which):
        remote(wall.at[chunk], wall.at[chunk], w_send.at[chunk, which], w_recv.at[chunk], seg=right).wait_send()

    def near_sent(k, carry):
        for which in range(3):
            sent(at(x, y_of(k), core), which)
        for i in (1, 2, 3):
            sent(at(x + i, y_of(k), core), 2)
        row = y_of(k)

        @pl.when(row < 2)
        def _():
            sent(at(x + 3, row, core), 0)

        @pl.when(row >= 2)
        def _():
            sent(at(x + 1, row, core), 1)

        return carry

    lax.fori_loop(0, 4, near_sent, 0)

    def given(i, carry):
        @pl.when(owner_of(i) != me)
        def _():
            remote(qmsg.at[i % 4], qin.at[me], q_send.at[i], q_recv.at[me], seg=right).wait_send()

        return carry

    lax.fori_loop(0, 8, given, 0)

    def out_given(i, carry):
        remote(ow_ref, ow_ref, o_send.at[i], o_recv.at[me], seg=right).wait_send()
        return carry

    lax.fori_loop(1, SEGS, out_given, 0)

    @pl.when(is_owner)
    def _():
        def answered(s, carry):
            @pl.when(s != me)
            def _():
                remote(zst.at[s], zbuf.at[slot], z_send.at[s], z_recv.at[slot], seg=right).wait_send()

            return carry

        lax.fori_loop(0, SEGS, answered, 0)

    def heads_given(i, carry):
        remote(heads.at[vid], heads.at[vid], h_send.at[i], h_recv.at[vid], video=vid).wait_send()
        return carry

    lax.fori_loop(1, GROUPS, heads_given, 0)


def per_device(
    tokens, prompt_ids, prompt_table, qkv_weight, out_weight, init_first, init_second, inner_rate
):
    vmem = pl.BlockSpec(memory_space=pltpu.VMEM)
    smem = pl.BlockSpec(memory_space=pltpu.SMEM)
    dma = pltpu.SemaphoreType.DMA
    mixed = pl.pallas_call(
        kernel,
        out_shape=jax.ShapeDtypeStruct((VIDEOS * ROWS, 192), bf16),
        in_specs=[smem, smem, pl.BlockSpec(memory_space=pl.ANY)] + [vmem] * 5,
        out_specs=vmem,
        scratch_shapes=[
            pltpu.VMEM((VIDEOS, ROWS, 3072), bf16),
            pltpu.VMEM((SEGS, VIDEOS * ROWS, 128), bf16),
            pltpu.VMEM((SEGS, 96, 384), bf16),
            pltpu.VMEM((VIDEOS * ROWS, 384), f32),
            pltpu.VMEM((4, 3, ROWS, 128), bf16),
            pltpu.VMEM((SEGS, 3, ROWS, 128), bf16),
            pltpu.VMEM((SEGS + 1, ROWS, 128), f32),
            pltpu.VMEM((8, ROWS, 128), f32),
            pltpu.VMEM((2048, 192), bf16),
            pltpu.VMEM((GROUPS, VIDEOS * ROWS, 128), bf16),
            pltpu.VMEM((HS, 256), bf16),
            pltpu.VMEM((HS, 256), bf16),
            dma,
            dma((SEGS, 3)),
            dma((SEGS,)),
            dma((3,)),
            dma((8,)),
            dma((SEGS,)),
            dma((SEGS,)),
            dma((SEGS,)),
            dma((SEGS,)),
            dma((8,)),
            dma((GROUPS,)),
            dma((GROUPS,)),
        ],
        compiler_params=pltpu.CompilerParams(
            collective_id=0, has_side_effects=True, vmem_limit_bytes=40 << 20
        ),
        name="chains",
    )(
        inner_rate,
        prompt_ids,
        tokens,
        prompt_table,
        qkv_weight.reshape(96, 384),
        out_weight,
        init_first,
        init_second,
    )
    return mixed.reshape(VIDEOS, ROWS, 192)


def solution(mesh):
    return jax.shard_map(
        per_device,
        mesh=mesh,
        in_specs=(
            P(None, "seg", None),
            P(None, "seg"),
            P(),
            P("seg", None, "video"),
            P("seg", "video"),
            P("video", None, None),
            P("video", None, None),
            P("video"),
        ),
        out_specs=P(None, "seg", "video"),
        check_vma=False,
    )
```

time: 1160 us -> 136 us (0.12)
  the two profiles are of different devices: /device:TPU:30 before, /device:TPU:64 now
where the time goes in v1:
time: 136 us
  Pallas kernels  131 us (96%)
  local copies, waits for them, and re-layouts  5.09 us (4%)
    pallas_call x1, Pallas kernels, per_device(): pl.pallas_call(kernel, out_shape=jax.ShapeDtypeStruct((VIDEOS * ROWS, 192...  131 us
    unnamed x16, local copies, waits for them, and re-layouts  5.08 us

profile of v1, /device:TPU:64, one launch (start us, length us, event | category | flops | bytes accessed | tf_op | source)
XLA Modules:
  0.0 135.7 jit_solution(13065529712355246187)
XLA Ops:
  0.0 0.0 copy-start
  0.0 0.0 copy-start.2
  0.0 0.8 copy.12.ids_ref
  0.8 0.1 copy-done
  0.9 0.0 copy-start.5
  0.9 0.0 copy-start.6
  0.9 0.0 copy-done.2
  0.9 0.7 copy-done.5
  1.7 0.0 copy-done.6
  1.7 0.0 copy-start.1
  1.7 1.1 copy-done.1
  2.8 0.0 copy-start.3
  2.8 0.8 copy-done.3
  3.6 0.0 copy-start.4
  3.6 0.8 copy-done.4
  4.5 130.6 %chains.1 = bf16[128,192]{1,0:T(8,128)(2,1)S(1)} custom-call(f32[2]{0:T(128)S(1)} %copy-done.6, s32[2,1]{1,0:T(2,128)S(1)} %copy.12.ids_ref, bf16[2,64,3072]{2,1,0:T(8,128)(2,1)S(1)} %copy-done.1, bf16[16,3072]{1,0:T(8,128)(2,1)S(1)} %copy-done.2, bf16[96,384]{1,0:T(8,128)(2,1)S(1)} %copy_bitcast_fusion.w_ref, bf16[64,192]{1,0:T(8,128)(2,1)S(1)} %copy-done.5, ...), custom_call_target="tpu_custom_call" | custom-call | tf_op jit(solution)/shard_map/chains/pallas_call | solution.py:459
  135.0 0.6 copy.16
  (1 shorter events, 0.0 us)
Async XLA Ops:
  0.0 0.9 copy-start
  0.0 0.9 copy-start.2
  0.9 0.8 copy-start.5
  0.9 0.8 copy-start.6
  1.7 1.1 copy-start.1
  2.8 0.8 copy-start.3
  3.6 0.8 copy-start.4

commit v2 on v1

v2 whole, which is shorter than its diff:
```python
import jax
import jax.numpy as jnp
from jax import lax
from jax.experimental import pallas as pl
from jax.experimental.pallas import tpu as pltpu
from jax.sharding import PartitionSpec as P

HS = 64
MINI = 16
SEGS = 32
GROUPS = 16
VIDEOS = 2
ROWS = 64
EPS = 1e-6
OWN = 4
WORKERS = SEGS - 2 * OWN
C0 = 0.7978845608028654
C1 = C0 * 0.044715
f32 = jnp.float32
bf16 = jnp.bfloat16


def contract(a, b, da, db):
    return lax.dot_general(a, b, (((da,), (db,)), ((), ())), preferred_element_type=f32)


def nn(a, b):
    return contract(a, b, 1, 0)


def nt(a, b):
    return contract(a, b, 1, 1)


def tn(a, b):
    return contract(a, b, 0, 0)


def gelu_parts(x):
    x2 = x * x
    t = jnp.tanh(x * (C0 + C1 * x2))
    half = 0.5 * x
    return half + half * t, t, x2, half


def gelu_slope(t, x2, half):
    return (0.5 + 0.5 * t) + half * (1.0 - t * t) * (C0 + (3.0 * C1) * x2)


def remote(src, dst, send, recv, seg=None, video=None):
    where = {"seg": seg} if video is None else {"video": video}
    return pltpu.make_async_remote_copy(
        src_ref=src,
        dst_ref=dst,
        send_sem=send,
        recv_sem=recv,
        device_id=where,
        device_id_type=pl.DeviceIdType.MESH,
    )


def arrived(ref, sem):
    pltpu.make_async_copy(ref, ref, sem).wait()


def tell(sem, **where):
    pl.semaphore_signal(sem, inc=1, device_id=where, device_id_type=pl.DeviceIdType.MESH)


def kernel(
    rate_ref,
    ids_ref,
    tok_ref,
    table_ref,
    w_ref,
    ow_ref,
    first_ref,
    second_ref,
    out_ref,
    tok,
    table,
    xin,
    wall,
    acc,
    qmsg,
    qin,
    zst,
    zbuf,
    ow,
    owall,
    heads,
    res,
    land,
    first,
    second,
    grads,
    q_pre,
    q_cross,
    tok_sem,
    table_sem,
    w_sem,
    state_sem,
    ow_sem,
    w_send,
    w_recv,
    q_send,
    q_recv,
    o_send,
    o_recv,
    z_send,
    z_recv,
    h_send,
    h_recv,
    a_recv,
    r_send,
    r_recv,
    ring_sem,
):
    me = lax.axis_index("seg")
    vid = lax.axis_index("video")
    core = me % 2
    chip = me // 2
    x = chip // 4
    y = chip % 4
    is_owner = jnp.logical_or(me < OWN, me >= SEGS - OWN)
    is_worker = jnp.logical_not(is_owner)
    head = me % 2

    def at(xx, yy, cc):
        return ((xx % 4) * 4 + yy) * 2 + cc

    loads = [
        pltpu.make_async_copy(w_ref.at[j], wall.at[me, :, pl.ds(128 * j, 128)], w_sem) for j in range(3)
    ]
    loads.append(pltpu.make_async_copy(tok_ref, tok, tok_sem))
    loads.append(pltpu.make_async_copy(table_ref, table, table_sem))
    loads.append(pltpu.make_async_copy(first_ref.at[head], first, state_sem.at[0]))
    loads.append(pltpu.make_async_copy(second_ref.at[head], second, state_sem.at[1]))
    loads.append(pltpu.make_async_copy(ow_ref, ow, ow_sem))
    for load in loads:
        load.start()

    right, left, mate = at(x + 1, y, core), at(x + 3, y, core), at(x, y, 1 - core)
    y1 = y + 1 - 2 * (y % 2)
    y2 = (y + 2) % 4
    y3 = 3 - y
    ring = (vid // 8) * 8
    upper = ring + (vid + 1) % 8
    lower = ring + (vid + 7) % 8
    across = (vid + 8) % 16

    barrier = pltpu.get_barrier_semaphore()
    for target in (at(x, y1, core), at(x, y2, core), at(x, y3, core), right, left, mate):
        tell(barrier, seg=target)

    @pl.when(is_worker)
    def _():
        for target in (upper, lower, across):
            tell(barrier, video=target)

    lane = lax.broadcasted_iota(jnp.int32, (16, 16), 1)
    picks = [jnp.where(lane == ids_ref[0, v], 1.0, 0.0).astype(bf16) for v in range(VIDEOS)]

    def prepare(g, carry):
        span = pl.ds(pl.multiple_of(g * 384, 128), 384)
        for v in range(VIDEOS):
            bias = nn(picks[v], table[:, span])[0:1]
            part = (tok[v, :, span].astype(f32) + bias).astype(bf16)
            for i in range(4):
                xin[g * 4 + i, ROWS * v : ROWS * (v + 1), 0:96] = part[:, 96 * i : 96 * (i + 1)]
        return carry

    loads[3].wait()
    loads[4].wait()
    lax.fori_loop(0, 8, prepare, 0)
    acc[...] = jnp.zeros_like(acc)
    arrived(wall.at[me], w_sem)
    pl.semaphore_wait(barrier, jnp.where(is_worker, 9, 6))

    def y_of(k):
        return jnp.where(k == 0, y, jnp.where(k == 1, y1, jnp.where(k == 2, y2, y3)))

    def pass_on(chunk, target):
        remote(wall.at[chunk], wall.at[chunk], w_send, w_recv.at[chunk], seg=target).start()

    for target in (right, left, at(x, y1, core), at(x, y2, core), at(x, y3, core), mate):
        pass_on(me, target)

    def landed(chunk):
        arrived(wall.at[chunk], w_recv.at[chunk])

    def add(chunk):
        acc[...] += nn(xin[chunk, :, 0:96], wall[chunk])

    def y_step(k, carry):
        chunk = at(x, y_of(k), core)
        landed(chunk)
        pass_on(chunk, right)
        pass_on(chunk, left)
        pass_on(chunk, mate)
        return carry

    def x_step(k, carry):
        @pl.when(k < 3)
        def _():
            y_step(k + 1, 0)

        row = y_of(k)
        a = at(x + 3, row, core)
        b = at(x + 1, row, core)
        landed(a)

        @pl.when(row < 2)
        def _():
            pass_on(a, right)

        pass_on(a, mate)
        landed(b)

        @pl.when(row >= 2)
        def _():
            pass_on(b, left)

        pass_on(b, mate)
        add(at(x, row, core))
        add(a)
        add(b)
        c = at(x, row, 1 - core)
        landed(c)
        add(c)
        return carry

    lax.fori_loop(0, 4, x_step, 0)

    def far_step(k, carry):
        row = y_of(k)
        a = at(x + 2, row, core)
        landed(a)
        pass_on(a, mate)
        add(a)
        for i in (1, 3):
            c = at(x + i, row, 1 - core)
            landed(c)
            add(c)
        return carry

    lax.fori_loop(0, 4, far_step, 0)

    def last_step(k, carry):
        c = at(x + 2, y_of(k), 1 - core)
        landed(c)
        add(c)
        return carry

    lax.fori_loop(0, 4, last_step, 0)

    low = lax.broadcasted_iota(jnp.int32, (1, 128), 1) < HS
    full = [acc[:, 128 * j : 128 * (j + 1)] for j in range(3)]
    turned = [pltpu.roll(part, HS, 1) for part in full]
    for v in range(VIDEOS):
        q, k, val = [part[ROWS * v : ROWS * (v + 1)] for part in full]
        qt, kt, vt = [part[ROWS * v : ROWS * (v + 1)] for part in turned]
        for h in range(2):
            kq = jnp.where(low, k, qt) if h == 0 else jnp.where(low, kt, q)
            kq = kq.astype(bf16)
            for back in range(2):
                n = 4 * back + 2 * v + h
                order = [3, 2, 1, 0] if back else [0, 1, 2, 3]
                for t in range(4):
                    o = order[t]
                    qmsg[n, MINI * t : MINI * (t + 1)] = kq[MINI * o : MINI * (o + 1)]
                for t in range(2):
                    o, p = order[t], order[t + 2]
                    one, two = slice(MINI * o, MINI * (o + 1)), slice(MINI * p, MINI * (p + 1))
                    pair = jnp.where(low, val[one], vt[two]) if h == 0 else jnp.where(low, vt[one], val[two])
                    qmsg[n, ROWS + MINI * t : ROWS + MINI * (t + 1)] = pair.astype(bf16)

    def give(i):
        owner = jnp.where(i < 4, i, SEGS - 8 + i)

        @pl.when(owner == me)
        def _():
            pltpu.make_async_copy(qmsg.at[i], qin.at[me], q_recv.at[me]).start()

        @pl.when(owner != me)
        def _():
            remote(qmsg.at[i], qin.at[me], q_send.at[i], q_recv.at[me], seg=owner).start()

    def given(i):
        @pl.when(jnp.where(i < 4, i, SEGS - 8 + i) != me)
        def _():
            remote(qmsg.at[i], qin.at[me], q_send.at[i], q_recv.at[me], seg=right).wait_send()

    def give_soon(n, carry):
        give(jnp.where(me < 16, n, n + 4))
        return carry

    def give_later(n, carry):
        give(jnp.where(me < 16, n + 4, n))
        return carry

    def soon_given(n, carry):
        given(jnp.where(me < 16, n, n + 4))
        return carry

    def later_given(n, carry):
        given(jnp.where(me < 16, n + 4, n))
        return carry

    lax.fori_loop(0, 4, give_soon, 0)

    @pl.when(is_worker)
    def _():
        lax.fori_loop(0, 4, soon_given, 0)

    lax.fori_loop(0, 4, give_later, 0)

    loads[-1].wait()
    my_rows = pl.ds(pl.multiple_of(me * 64, 64), 64)

    def give_out_weight(i):
        target = OWN + (i + me) % WORKERS
        remote(ow, owall.at[my_rows], o_send, o_recv, seg=target).start()

    def piece_place(s, t):
        upper_half = jnp.where(s < 16, 0, 1)
        i = jnp.where(s < 16, 4 * s + t, 4 * (SEGS - 1 - s) + 3 - t)
        p = i % 12
        return OWN + 12 * upper_half + (p % 6) * 2 + p // 6, i // 12

    @pl.when(is_owner)
    def _():
        back = jnp.where(me < OWN, 0, 1)
        slot = jnp.where(me < OWN, me, me - (SEGS - 8))
        eta = rate_ref[head]
        loads[5].wait()
        loads[6].wait()

        def seg_of(j):
            return j + back * (SEGS - 1 - 2 * j)

        def give_answer(j, t):
            s = seg_of(j)
            target, place = piece_place(s, t + back * (3 - 2 * t))
            remote(zst.at[j, t], zbuf.at[place, slot], z_send, z_recv.at[place], seg=target).start()

        grads[...] = jnp.zeros_like(grads)
        q_pre[...] = jnp.zeros_like(q_pre)
        q_cross[...] = jnp.zeros_like(q_cross)

        def wait_for(j):
            s = seg_of(j)
            arrived(qin.at[s], q_recv.at[s])

        def segment(j, pre, begin=False, end=False):
            if not end:
                wait_for(j + 1)
            before = j if begin else j - 1
            s, s_before, s_next = seg_of(j), seg_of(before), seg_of(j if end else j + 1)
            keys = qin[s, 0:ROWS, 0:HS]
            queries = qin[s, 0:ROWS, HS:128]
            values = jnp.concatenate([qin[s, ROWS:96, 0:HS], qin[s, ROWS:96, HS:128]], 0)
            keys_before = qin[s_before, 0:ROWS, 0:HS]
            last_query = qin[s_before, 48:ROWS, HS:128]
            keys_ahead = jnp.concatenate([keys[MINI:], qin[s_next, 0:MINI, 0:HS]], 0)
            grads_before = grads[...]
            layer_one = (first[...].astype(f32) - eta * tn(keys_before, grads_before)).astype(bf16)
            first[...] = layer_one
            pre_q = q_pre[...] + nn(q_cross[...], grads_before)
            base_k = nn(keys_ahead, layer_one)
            base_q = nn(queries, layer_one)
            cross = -eta * nt(keys_ahead, keys)
            cross_b = cross.astype(bf16)
            cross_q = (-eta * nt(queries, keys)).astype(bf16)
            targets = values.astype(f32) - keys.astype(f32)
            targets = targets - jnp.mean(targets, -1, keepdims=True)
            layer_two = second[...].astype(f32)
            mu = jnp.mean(layer_two, 0, keepdims=True)
            centred = layer_two - mu
            ahead = [base_k[MINI * t : MINI * (t + 1)] for t in range(4)]
            done = []
            for t in range(4):
                rows = slice(MINI * t, MINI * (t + 1))
                h, th, x2, half = gelu_parts(pre)
                hb = h.astype(bf16)
                weights = centred.astype(bf16)
                target = targets[rows]
                c = nt(hb, weights)
                w = nn(target.astype(bf16), weights)
                u = nn(c.astype(bf16), weights)
                rho = lax.rsqrt(jnp.mean(c * c, -1, keepdims=True) + EPS)
                m = jnp.mean(target * c, -1, keepdims=True)
                r2 = rho * rho
                b = rho * (1.0 / MINI)
                a = (r2 * (1.0 / MINI)) * (EPS * r2 + rho * m)
                ct = nt(weights, hb)
                target_t = target.T
                rho_t = lax.rsqrt(jnp.sum(ct * ct, 0, keepdims=True) * (1.0 / HS) + EPS)
                m_t = jnp.sum(target_t * ct, 0, keepdims=True) * (1.0 / HS)
                r2_t = rho_t * rho_t
                b_t = rho_t * (eta / MINI)
                a_t = (r2_t * (-eta / MINI)) * (EPS * r2_t + rho_t * m_t)
                moved = centred + nn((a_t * ct + b_t * target_t).astype(bf16), hb)
                slope = gelu_slope(th, x2, half)
                grad = a * (u * slope) - b * (w * slope)
                grad_b = grad.astype(bf16)
                done.append(grad_b)
                sums = [ahead[t], None]
                for i in range(MINI):
                    col = cross[rows, MINI * t + i : MINI * t + i + 1]
                    term = jnp.broadcast_to(col, (MINI, 256)) * jnp.broadcast_to(grad[i : i + 1], (MINI, 256))
                    sums[i % 2] = term if sums[i % 2] is None else sums[i % 2] + term
                pre = sums[0] + sums[1]
                for r in range(t + 1, 4):
                    ahead[r] = ahead[r] + nn(cross_b[MINI * r : MINI * (r + 1), rows], grad_b)
                hq = gelu_parts(pre_q)[0]
                cq = nt(hq.astype(bf16), weights)
                rho_q = lax.rsqrt(jnp.mean(cq * cq, -1, keepdims=True) + EPS)
                if t == 0:
                    zst[before, 3, :, 0:HS] = last_query.astype(f32) + cq * rho_q
                else:
                    zst[j, t - 1, :, 0:HS] = queries[MINI * (t - 1) : MINI * t].astype(f32) + cq * rho_q
                if t < 3:
                    so_far = jnp.concatenate(done, 0) if t else grad_b
                    pre_q = base_q[rows] + nn(cross_q[rows, : MINI * (t + 1)], so_far)
                centred = moved
            grads[...] = jnp.concatenate(done, 0)
            q_pre[...] = base_q[48:ROWS]
            q_cross[...] = cross_q[48:ROWS]
            second[...] = (centred + mu).astype(bf16)
            if not begin:
                give_answer(before, 3)
            for t in range(3):
                give_answer(j, t)
            return pre

        def send_out_weight(i, carry):
            give_out_weight(i)
            return carry

        lax.fori_loop(0, WORKERS, send_out_weight, 0)
        wait_for(0)
        pre = nn(qin[seg_of(0), 0:MINI, 0:HS], first[...])
        pre = segment(0, pre, begin=True)
        pre = lax.fori_loop(1, SEGS - 1, segment, pre)
        segment(SEGS - 1, pre, end=True)
        pre_q = q_pre[...] + nn(q_cross[...], grads[...])
        layer_two = second[...].astype(f32)
        centred = (layer_two - jnp.mean(layer_two, 0, keepdims=True)).astype(bf16)
        c = nt(gelu_parts(pre_q)[0].astype(bf16), centred)
        rho = lax.rsqrt(jnp.mean(c * c, -1, keepdims=True) + EPS)
        zst[SEGS - 1, 3, :, 0:HS] = qin[seg_of(SEGS - 1), 48:ROWS, HS:128].astype(f32) + c * rho
        give_answer(SEGS - 1, 3)

    @pl.when(is_worker)
    def _():
        lax.fori_loop(0, 4, later_given, 0)

        def send_out_weight(i, carry):
            @pl.when(OWN + (i + me) % WORKERS != me)
            def _():
                give_out_weight(i)

            return carry

        lax.fori_loop(0, WORKERS, send_out_weight, 0)
        pltpu.make_async_copy(ow, owall.at[my_rows], o_recv).start()

        for k in range(3):
            tell(ring_sem.at[k], video=upper)
            tell(ring_sem.at[k], video=lower)
            pl.semaphore_wait(ring_sem.at[k], 2)
        tell(ring_sem.at[3], video=across)
        pl.semaphore_wait(ring_sem.at[3], 1)

        arrived(owall, o_recv)
        upper_half = jnp.where(me < 16, 0, 1)
        r = me - OWN - 12 * upper_half
        p = r // 2 + 6 * (r % 2)
        count = jnp.where(p < 4, 6, 5)
        mine = pl.ds(pl.multiple_of(vid * 128, 128), 128)
        theirs = pl.ds(pl.multiple_of(across * 128, 128), 128)

        def place_of(n):
            place = count - 1 - n
            i = 12 * place + p
            s = jnp.where(upper_half == 0, i // 4, SEGS - 1 - i // 4)
            t = jnp.where(upper_half == 0, i % 4, 3 - i % 4)
            return place, s, t

        def spread(place, columns):
            block = heads.at[place, :, columns]

            def one(d, carry):
                remote(
                    block, block, h_send.at[place], h_recv.at[place], video=ring + (vid + d) % 8
                ).start()
                return carry

            lax.fori_loop(1, 8, one, 0)

        def gather(n):
            place, _, _ = place_of(n)
            arrived(zbuf.at[place], z_recv.at[place])
            for v in range(VIDEOS):
                pair = [zbuf[place, 2 * v + h, :, 0:HS] + zbuf[place, 4 + 2 * v + h, :, 0:HS] for h in range(2)]
                heads[place, MINI * v : MINI * (v + 1), mine] = jnp.concatenate(pair, 1).astype(bf16)
            block = heads.at[place, :, mine]
            remote(block, block, h_send.at[place], a_recv.at[place], video=across).start()
            spread(place, mine)

        def relay(n):
            place, _, _ = place_of(n)
            arrived(heads.at[place, :, theirs], a_recv.at[place])
            spread(place, theirs)

        def finish(n):
            place, s, t = place_of(n)
            arrived(heads.at[place, :, pl.ds(0, 128 * 14)], h_recv.at[place])
            res[place] = nn(heads[place], owall[...]).astype(bf16)

            @pl.when(s == me)
            def _():
                pltpu.make_async_copy(res.at[place], land.at[t], r_recv).start()

            @pl.when(s != me)
            def _():
                remote(res.at[place], land.at[t], r_send.at[place], r_recv, seg=s).start()

        def piece(n, carry):
            relay(n - 1)
            gather(n)
            finish(n - 1)
            return carry

        gather(0)
        lax.fori_loop(1, count, piece, 0)
        relay(count - 1)
        finish(count - 1)

        def piece_sent(n, carry):
            i = 12 * n + p
            s = jnp.where(upper_half == 0, i // 4, SEGS - 1 - i // 4)
            arrived(heads.at[n, :, pl.ds(0, 128 * (GROUPS - 1))], h_send.at[n])

            @pl.when(s != me)
            def _():
                remote(res.at[n], land.at[0], r_send.at[n], r_recv, seg=s).wait_send()

            return carry

        lax.fori_loop(0, count, piece_sent, 0)
        arrived(owall.at[pl.ds(0, 64 * (WORKERS - 1))], o_send)
        loads[5].wait()
        loads[6].wait()

    @pl.when(is_owner)
    def _():
        lax.fori_loop(0, 4, soon_given, 0)
        lax.fori_loop(0, 4, later_given, 0)
        arrived(owall.at[pl.ds(0, 64 * WORKERS)], o_send)
        arrived(zst, z_send)

    arrived(wall.at[pl.ds(0, SEGS - 1)], w_send)

    arrived(land, r_recv)
    for t in range(4):
        for v in range(VIDEOS):
            out_ref[v, MINI * t : MINI * (t + 1)] = land[t, MINI * v : MINI * (v + 1)]


def per_device(
    tokens, prompt_ids, prompt_table, qkv_weight, out_weight, init_first, init_second, inner_rate
):
    vmem = pl.BlockSpec(memory_space=pltpu.VMEM)
    smem = pl.BlockSpec(memory_space=pltpu.SMEM)
    hbm = pl.BlockSpec(memory_space=pltpu.HBM)
    dma = pltpu.SemaphoreType.DMA
    return pl.pallas_call(
        kernel,
        out_shape=jax.ShapeDtypeStruct((VIDEOS, ROWS, 192), bf16),
        in_specs=[smem, smem] + [hbm] * 6,
        out_specs=vmem,
        scratch_shapes=[
            pltpu.VMEM((VIDEOS, ROWS, 3072), bf16),
            pltpu.VMEM((16, 3072), bf16),
            pltpu.VMEM((SEGS, VIDEOS * ROWS, 128), bf16),
            pltpu.VMEM((SEGS, 96, 384), bf16),
            pltpu.VMEM((VIDEOS * ROWS, 384), f32),
            pltpu.VMEM((8, 96, 128), bf16),
            pltpu.VMEM((SEGS, 96, 128), bf16),
            pltpu.VMEM((SEGS, 4, MINI, 128), f32),
            pltpu.VMEM((6, 8, MINI, 128), f32),
            pltpu.VMEM((64, 192), bf16),
            pltpu.VMEM((2048, 192), bf16),
            pltpu.VMEM((6, VIDEOS * MINI, 2048), bf16),
            pltpu.VMEM((6, VIDEOS * MINI, 192), bf16),
            pltpu.VMEM((4, VIDEOS * MINI, 192), bf16),
            pltpu.VMEM((HS, 256), bf16),
            pltpu.VMEM((HS, 256), bf16),
            pltpu.VMEM((ROWS, 256), bf16),
            pltpu.VMEM((MINI, 256), f32),
            pltpu.VMEM((MINI, HS), bf16),
            dma,
            dma,
            dma,
            dma((2,)),
            dma,
            dma,
            dma((SEGS,)),
            dma((8,)),
            dma((SEGS,)),
            dma,
            dma,
            dma,
            dma((6,)),
            dma((6,)),
            dma((6,)),
            dma((6,)),
            dma((6,)),
            dma,
            pltpu.SemaphoreType.REGULAR((4,)),
        ],
        compiler_params=pltpu.CompilerParams(
            collective_id=0, has_side_effects=True, vmem_limit_bytes=60 << 20
        ),
        name="chains",
    )(
        inner_rate,
        prompt_ids.T,
        tokens,
        prompt_table,
        jnp.transpose(qkv_weight, (1, 0, 2)),
        out_weight,
        init_first,
        init_second,
    )


def solution(mesh):
    return jax.shard_map(
        per_device,
        mesh=mesh,
        in_specs=(
            P(None, "seg", None),
            P(None, "seg"),
            P(),
            P("seg", None, "video"),
            P("seg", "video"),
            P("video", None, None),
            P("video", None, None),
            P("video"),
        ),
        out_specs=P(None, "seg", "video"),
        check_vma=False,
    )
```

time: 136 us -> 116 us (0.85)
  the two profiles are of different devices: /device:TPU:64 before, /device:TPU:1 now
where the time goes in v2:
time: 116 us; the launch traced here: 113 us
  Pallas kernels  112 us (97%)
  local copies, waits for them, and re-layouts  1.47 us (1%)
    pallas_call x1, Pallas kernels, per_device(): pl.pallas_call(kernel, out_shape=jax.ShapeDtypeStruct((VIDEOS, ROWS, 192)...  112 us

profile of v2, /device:TPU:1, one launch (start us, length us, event | category | flops | bytes accessed | tf_op | source)
XLA Modules:
  0.0 113.3 jit_solution(1310477572509163483)
XLA Ops:
  0.0 111.9 %chains.1 = bf16[2,64,192]{2,1,0:T(8,128)(2,1)} custom-call(f32[2]{0:T(128)} %rate_ref.1, s32[1,2]{1,0:T(1,128)} %bitcast.3, bf16[2,64,3072]{2,1,0:T(8,128)(2,1)} %tok_ref.1, bf16[16,3072]{1,0:T(8,128)(2,1)} %table_ref.1, bf16[3,96,128]{2,1,0:T(8,128)(2,1)} %bitcast.2, bf16[64,192]{1,0:T(8,128)(2,1)} %ow_ref.1, bf16[2,64,256]{2,1,0:T(8,128)(2,1)} %first_ref.1, ...), custom_call_target="tpu_custom_call" | custom-call | tf_op jit(solution)/shard_map/chains/pallas_call | solution.py:579
  111.9 1.5 %copy.10 = bf16[2,64,192]{2,1,0:T(8,128)(2,1)} copy(bf16[2,64,192]{2,1,0:T(8,128)(2,1)} %chains.1) | data formatting | bytes 98304

commit v3 on v2

--- a/solution.py
+++ b/solution.py
@@ -14,6 +14,8 @@
 EPS = 1e-6
 OWN = 4
 WORKERS = SEGS - 2 * OWN
+PARTS = 1
+PART = 96 // PARTS
 C0 = 0.7978845608028654
 C1 = C0 * 0.044715
 f32 = jnp.float32
@@ -94,8 +96,11 @@
     first,
     second,
     grads,
-    q_pre,
-    q_cross,
+    q_weights,
+    p_query,
+    p_target,
+    p_across,
+    p_turned,
     tok_sem,
     table_sem,
     w_sem,
@@ -180,82 +185,107 @@
     def y_of(k):
         return jnp.where(k == 0, y, jnp.where(k == 1, y1, jnp.where(k == 2, y2, y3)))
 
-    def pass_on(chunk, target):
-        remote(wall.at[chunk], wall.at[chunk], w_send, w_recv.at[chunk], seg=target).start()
-
-    for target in (right, left, at(x, y1, core), at(x, y2, core), at(x, y3, core), mate):
-        pass_on(me, target)
-
-    def landed(chunk):
-        arrived(wall.at[chunk], w_recv.at[chunk])
+    def half_of(chunk, part):
+        return wall.at[chunk, pl.ds(PART * part, PART)]
+
+    def pass_on(chunk, part, target):
+        block = half_of(chunk, part)
+        remote(block, block, w_send, w_recv.at[chunk, part], seg=target).start()
+
+    def start_lines(part):
+        for target in (at(x, y1, core), at(x, y2, core), at(x, y3, core)):
+            pass_on(me, part, target)
+
+    start_lines(0)
+    for part in range(PARTS):
+        pass_on(me, part, right)
+        pass_on(me, part, left)
+
+    def landed(chunk, part):
+        arrived(half_of(chunk, part), w_recv.at[chunk, part])
 
     def add(chunk):
         acc[...] += nn(xin[chunk, :, 0:96], wall[chunk])
 
-    def y_step(k, carry):
-        chunk = at(x, y_of(k), core)
-        landed(chunk)
-        pass_on(chunk, right)
-        pass_on(chunk, left)
-        pass_on(chunk, mate)
-        return carry
-
-    def x_step(k, carry):
-        @pl.when(k < 3)
-        def _():
-            y_step(k + 1, 0)
-
+    def y_step(part):
+        def one(k, carry):
+            chunk = at(x, y_of(k), core)
+            landed(chunk, part)
+            pass_on(chunk, part, right)
+            pass_on(chunk, part, left)
+            pass_on(chunk, part, mate)
+            return carry
+
+        one(1, 0)
+        if part + 1 < PARTS:
+            start_lines(part + 1)
+        pass_on(me, part, mate)
+        lax.fori_loop(2, 4, one, 0)
+
+    def x_step(k, part):
         row = y_of(k)
         a = at(x + 3, row, core)
         b = at(x + 1, row, core)
-        landed(a)
-
-        @pl.when(row < 2)
+        landed(a, part)
+        to_right = (row + part) % 2 == 0
+
+        @pl.when(to_right)
         def _():
-            pass_on(a, right)
-
-        pass_on(a, mate)
-        landed(b)
-
-        @pl.when(row >= 2)
+            pass_on(a, part, right)
+
+        pass_on(a, part, mate)
+        landed(b, part)
+
+        @pl.when(jnp.logical_not(to_right))
         def _():
-            pass_on(b, left)
-
-        pass_on(b, mate)
-        add(at(x, row, core))
-        add(a)
-        add(b)
-        c = at(x, row, 1 - core)
-        landed(c)
-        add(c)
+            pass_on(b, part, left)
+
+        pass_on(b, part, mate)
+
+    def add_near(k, carry):
+        add(at(x, y_of(k), core))
+        add(at(x + 3, y_of(k), core))
+        add(at(x + 1, y_of(k), core))
         return carry
 
-    lax.fori_loop(0, 4, x_step, 0)
+    for part in range(PARTS):
+        y_step(part)
+        x_step(0, part)
+
+        if part > 0:
+            lax.fori_loop(1, 4, lambda k, c: (x_step(k, part - 1), c)[1], 0)
+    lax.fori_loop(1, 4, lambda k, c: (x_step(k, PARTS - 1), c)[1], 0)
+    lax.fori_loop(0, 4, add_near, 0)
+
+    def other_add(chunk):
+        for part in range(PARTS):
+            landed(chunk, part)
+        add(chunk)
 
     def far_step(k, carry):
-        row = y_of(k)
-        a = at(x + 2, row, core)
-        landed(a)
-        pass_on(a, mate)
-        add(a)
-        for i in (1, 3):
-            c = at(x + i, row, 1 - core)
-            landed(c)
-            add(c)
+        far = at(x + 2, y_of(k), core)
+        for part in range(PARTS):
+            landed(far, part)
+            pass_on(far, part, mate)
+        add(far)
+        for i in (0, 1, 3):
+            other_add(at(x + i, y_of(k), 1 - core))
         return carry
 
     lax.fori_loop(0, 4, far_step, 0)
 
     def last_step(k, carry):
-        c = at(x + 2, y_of(k), 1 - core)
-        landed(c)
-        add(c)
+        other_add(at(x + 2, y_of(k), 1 - core))
         return carry
 
     lax.fori_loop(0, 4, last_step, 0)
 
     low = lax.broadcasted_iota(jnp.int32, (1, 128), 1) < HS
-    full = [acc[:, 128 * j : 128 * (j + 1)] for j in range(3)]
+    full = [acc[:, 128 * j : 128 * (j + 1)].astype(bf16).astype(f32) for j in range(3)]
+    wanted = full[2] - full[1]
+    mean_low = jnp.sum(jnp.where(low, wanted, 0.0), -1, keepdims=True) * (1.0 / HS)
+    mean_high = jnp.sum(jnp.where(low, 0.0, wanted), -1, keepdims=True) * (1.0 / HS)
+    full[2] = wanted - jnp.where(low, mean_low, mean_high)
     turned = [pltpu.roll(part, HS, 1) for part in full]
     for v in range(VIDEOS):
         q, k, val = [part[ROWS * v : ROWS * (v + 1)] for part in full]
@@ -345,35 +375,58 @@
             remote(zst.at[j, t], zbuf.at[place, slot], z_send, z_recv.at[place], seg=target).start()
 
         grads[...] = jnp.zeros_like(grads)
-        q_pre[...] = jnp.zeros_like(q_pre)
-        q_cross[...] = jnp.zeros_like(q_cross)
+        row_block = lax.broadcasted_iota(jnp.int32, (ROWS, ROWS), 0) // MINI
+        upto = row_block >= lax.broadcasted_iota(jnp.int32, (ROWS, ROWS), 1) // MINI
 
         def wait_for(j):
             s = seg_of(j)
             arrived(qin.at[s], q_recv.at[s])
 
-        def segment(j, pre, begin=False, end=False):
+        def lay_out(j, slot):
+            s = seg_of(j)
+            keys = qin[s, 0:ROWS, 0:HS]
+            targets = jnp.concatenate([qin[s, ROWS:96, 0:HS], qin[s, ROWS:96, HS:128]], 0)
+            p_query[slot] = qin[s, 0:ROWS, HS:128]
+            p_turned[slot] = keys.T
+            targets = targets.astype(f32)
+            p_target[slot] = targets
+            for t in range(4):
+                p_across[slot, t] = targets[MINI * t : MINI * (t + 1)].T
+
+        def query_hidden(slot, keys, layer_one, grad):
+            queries = p_query[slot]
+            cross = jnp.where(upto, -eta * nt(queries, keys), 0.0).astype(bf16)
+            return gelu_parts(nn(queries, layer_one) + nn(cross, grad))[0].astype(bf16)
+
+        def query_answers(slot, h, j, which):
+            for t in which:
+                rows = slice(MINI * t, MINI * (t + 1))
+                c = nt(h[rows], q_weights[slot, t])
+                rho = lax.rsqrt(jnp.mean(c * c, -1, keepdims=True) + EPS)
+                zst[j, t, :, 0:HS] = p_query[slot, rows].astype(f32) + c * rho
+
+        def answer_queries(slot, keys, layer_one, grad, j):
+            query_answers(slot, query_hidden(slot, keys, layer_one, grad), j, range(4))
+
+        def segment(j, pre, slot, begin=False, end=False):
             if not end:
                 wait_for(j + 1)
-            before = j if begin else j - 1
-            s, s_before, s_next = seg_of(j), seg_of(before), seg_of(j if end else j + 1)
+            s, s_next = seg_of(j), seg_of(j if end else j + 1)
             keys = qin[s, 0:ROWS, 0:HS]
-            queries = qin[s, 0:ROWS, HS:128]
-            values = jnp.concatenate([qin[s, ROWS:96, 0:HS], qin[s, ROWS:96, HS:128]], 0)
-            keys_before = qin[s_before, 0:ROWS, 0:HS]
-            last_query = qin[s_before, 48:ROWS, HS:128]
+            targets = p_target[slot]
+            targets_t = [p_across[slot, t] for t in range(4)]
             keys_ahead = jnp.concatenate([keys[MINI:], qin[s_next, 0:MINI, 0:HS]], 0)
             grads_before = grads[...]
-            layer_one = (first[...].astype(f32) - eta * tn(keys_before, grads_before)).astype(bf16)
-            first[...] = layer_one
-            pre_q = q_pre[...] + nn(q_cross[...], grads_before)
+            layer_one = first[...]
+            if not begin:
+                before = j - 1
+                keys_before = qin[seg_of(before), 0:ROWS, 0:HS]
+                layer_before = layer_one
+                layer_one = (layer_one.astype(f32) - eta * nn(p_turned[1 - slot], grads_before)).astype(bf16)
+                first[...] = layer_one
             base_k = nn(keys_ahead, layer_one)
-            base_q = nn(queries, layer_one)
             cross = -eta * nt(keys_ahead, keys)
             cross_b = cross.astype(bf16)
-            cross_q = (-eta * nt(queries, keys)).astype(bf16)
-            targets = values.astype(f32) - keys.astype(f32)
-            targets = targets - jnp.mean(targets, -1, keepdims=True)
             layer_two = second[...].astype(f32)
             mu = jnp.mean(layer_two, 0, keepdims=True)
             centred = layer_two - mu
@@ -394,7 +447,7 @@
                 b = rho * (1.0 / MINI)
                 a = (r2 * (1.0 / MINI)) * (EPS * r2 + rho * m)
                 ct = nt(weights, hb)
-                target_t = target.T
+                target_t = targets_t[t]
                 rho_t = lax.rsqrt(jnp.sum(ct * ct, 0, keepdims=True) * (1.0 / HS) + EPS)
                 m_t = jnp.sum(target_t * ct, 0, keepdims=True) * (1.0 / HS)
                 r2_t = rho_t * rho_t
@@ -413,25 +466,25 @@
                 pre = sums[0] + sums[1]
                 for r in range(t + 1, 4):
                     ahead[r] = ahead[r] + nn(cross_b[MINI * r : MINI * (r + 1), rows], grad_b)
-                hq = gelu_parts(pre_q)[0]
-                cq = nt(hq.astype(bf16), weights)
-                rho_q = lax.rsqrt(jnp.mean(cq * cq, -1, keepdims=True) + EPS)
-                if t == 0:
-                    zst[before, 3, :, 0:HS] = last_query.astype(f32) + cq * rho_q
-                else:
-                    zst[j, t - 1, :, 0:HS] = queries[MINI * (t - 1) : MINI * t].astype(f32) + cq * rho_q
-                if t < 3:
-                    so_far = jnp.concatenate(done, 0) if t else grad_b
-                    pre_q = base_q[rows] + nn(cross_q[rows, : MINI * (t + 1)], so_far)
+                q_weights[slot, t] = moved.astype(bf16)
                 centred = moved
+                if t == 0 and not begin:
+                    h_query = query_hidden(1 - slot, keys_before, layer_before, grads_before)
+                if t == 0 and not begin:
+                    query_answers(1 - slot, h_query, before, [0])
+                if t == 1 and not begin:
+                    query_answers(1 - slot, h_query, before, [1])
+                if t == 2 and not begin:
+                    query_answers(1 - slot, h_query, before, [2])
+                if t == 3 and not begin:
+                    query_answers(1 - slot, h_query, before, [3])
             grads[...] = jnp.concatenate(done, 0)
-            q_pre[...] = base_q[48:ROWS]
-            q_cross[...] = cross_q[48:ROWS]
             second[...] = (centred + mu).astype(bf16)
+            if not end:
+                lay_out(j + 1, 1 - slot)
             if not begin:
-                give_answer(before, 3)
-            for t in range(3):
-                give_answer(j, t)
+                for t in range(4):
+                    give_answer(before, t)
             return pre
 
         def send_out_weight(i, carry):
@@ -441,16 +494,19 @@
         lax.fori_loop(0, WORKERS, send_out_weight, 0)
         wait_for(0)
         pre = nn(qin[seg_of(0), 0:MINI, 0:HS], first[...])
-        pre = segment(0, pre, begin=True)
-        pre = lax.fori_loop(1, SEGS - 1, segment, pre)
-        segment(SEGS - 1, pre, end=True)
-        pre_q = q_pre[...] + nn(q_cross[...], grads[...])
-        layer_two = second[...].astype(f32)
-        centred = (layer_two - jnp.mean(layer_two, 0, keepdims=True)).astype(bf16)
-        c = nt(gelu_parts(pre_q)[0].astype(bf16), centred)
-        rho = lax.rsqrt(jnp.mean(c * c, -1, keepdims=True) + EPS)
-        zst[SEGS - 1, 3, :, 0:HS] = qin[seg_of(SEGS - 1), 48:ROWS, HS:128].astype(f32) + c * rho
-        give_answer(SEGS - 1, 3)
+        lay_out(0, 0)
+        pre = segment(0, pre, 0, begin=True)
+
+        def two_segments(i, pre):
+            pre = segment(2 * i + 1, pre, 1)
+            return segment(2 * i + 2, pre, 0)
+
+        pre = lax.fori_loop(0, SEGS // 2 - 1, two_segments, pre)
+        segment(SEGS - 1, pre, 1, end=True)
+        s_last = seg_of(SEGS - 1)
+        answer_queries(1, qin[s_last, 0:ROWS, 0:HS], first[...], grads[...], SEGS - 1)
+        for t in range(4):
+            give_answer(SEGS - 1, t)
 
     @pl.when(is_worker)
     def _():
@@ -599,15 +655,18 @@
             pltpu.VMEM((HS, 256), bf16),
             pltpu.VMEM((HS, 256), bf16),
             pltpu.VMEM((ROWS, 256), bf16),
-            pltpu.VMEM((MINI, 256), f32),
-            pltpu.VMEM((MINI, HS), bf16),
+            pltpu.VMEM((2, 4, HS, 256), bf16),
+            pltpu.VMEM((2, ROWS, HS), bf16),
+            pltpu.VMEM((2, ROWS, HS), f32),
+            pltpu.VMEM((2, 4, HS, MINI), f32),
+            pltpu.VMEM((2, HS, ROWS), bf16),
             dma,
             dma,
             dma,
             dma((2,)),
             dma,
             dma,
-            dma((SEGS,)),
+            dma((SEGS, PARTS)),
             dma((8,)),
             dma((SEGS,)),
             dma,

time: 116 us -> 118 us (1.017)
  the two profiles are of different devices: /device:TPU:1 before, /device:TPU:64 now
where the time goes in v3:
time: 118 us
  Pallas kernels  116 us (98%)
  local copies, waits for them, and re-layouts  1.47 us (1%)
    pallas_call x1, Pallas kernels, per_device(): pl.pallas_call(kernel, out_shape=jax.ShapeDtypeStruct((VIDEOS, ROWS, 192)...  116 us

profile of v3, /device:TPU:64, one launch (start us, length us, event | category | flops | bytes accessed | tf_op | source)
XLA Modules:
  0.0 117.5 jit_solution(3291590051975175630)
XLA Ops:
  0.0 116.0 %chains.1 = bf16[2,64,192]{2,1,0:T(8,128)(2,1)} custom-call(f32[2]{0:T(128)} %rate_ref.1, s32[1,2]{1,0:T(1,128)} %bitcast.3, bf16[2,64,3072]{2,1,0:T(8,128)(2,1)} %tok_ref.1, bf16[16,3072]{1,0:T(8,128)(2,1)} %table_ref.1, bf16[3,96,128]{2,1,0:T(8,128)(2,1)} %bitcast.2, bf16[64,192]{1,0:T(8,128)(2,1)} %ow_ref.1, bf16[2,64,256]{2,1,0:T(8,128)(2,1)} %first_ref.1, ...), custom_call_target="tpu_custom_call" | custom-call | tf_op jit(solution)/shard_map/chains/pallas_call | solution.py:635
  116.1 1.5 %copy.10 = bf16[2,64,192]{2,1,0:T(8,128)(2,1)} copy(bf16[2,64,192]{2,1,0:T(8,128)(2,1)} %chains.1) | data formatting | bytes 98304

commit v4 on v3

--- a/solution.py
+++ b/solution.py
@@ -529,7 +529,6 @@
         tell(ring_sem.at[3], video=across)
         pl.semaphore_wait(ring_sem.at[3], 1)
 
-        arrived(owall, o_recv)
         upper_half = jnp.where(me < 16, 0, 1)
         r = me - OWN - 12 * upper_half
         p = r // 2 + 6 * (r % 2)
@@ -584,14 +583,24 @@
                 remote(res.at[place], land.at[t], r_send.at[place], r_recv, seg=s).start()
 
         def piece(n, carry):
-            relay(n - 1)
+            relay(n - 2)
             gather(n)
-            finish(n - 1)
+
+            @pl.when(n >= 4)
+            def _():
+                finish(n - 4)
+
             return carry
 
         gather(0)
-        lax.fori_loop(1, count, piece, 0)
+        gather(1)
+        arrived(owall, o_recv)
+        lax.fori_loop(2, count, piece, 0)
+        relay(count - 2)
+        finish(count - 4)
+        finish(count - 3)
         relay(count - 1)
+        finish(count - 2)
         finish(count - 1)
 
         def piece_sent(n, carry):

time: 118 us -> 102 us (0.86)
  the two profiles are of different devices: /device:TPU:64 before, /device:TPU:1 now
where the time goes in v4:
time: 102 us; the launch traced here: 100 us
  Pallas kernels  98.9 us (97%)
  local copies, waits for them, and re-layouts  1.47 us (1%)
    pallas_call x1, Pallas kernels, per_device(): pl.pallas_call(kernel, out_shape=jax.ShapeDtypeStruct((VIDEOS, ROWS, 192)...  98.9 us

profile of v4, /device:TPU:1, one launch (start us, length us, event | category | flops | bytes accessed | tf_op | source)
XLA Modules:
  0.0 100.4 jit_solution(15254189450654670998)
XLA Ops:
  0.0 98.9 %chains.1 = bf16[2,64,192]{2,1,0:T(8,128)(2,1)} custom-call(f32[2]{0:T(128)} %rate_ref.1, s32[1,2]{1,0:T(1,128)} %bitcast.3, bf16[2,64,3072]{2,1,0:T(8,128)(2,1)} %tok_ref.1, bf16[16,3072]{1,0:T(8,128)(2,1)} %table_ref.1, bf16[3,96,128]{2,1,0:T(8,128)(2,1)} %bitcast.2, bf16[64,192]{1,0:T(8,128)(2,1)} %ow_ref.1, bf16[2,64,256]{2,1,0:T(8,128)(2,1)} %first_ref.1, ...), custom_call_target="tpu_custom_call" | custom-call | tf_op jit(solution)/shard_map/chains/pallas_call | solution.py:644
  98.9 1.5 %copy.10 = bf16[2,64,192]{2,1,0:T(8,128)(2,1)} copy(bf16[2,64,192]{2,1,0:T(8,128)(2,1)} %chains.1) | data formatting | bytes 98304

commit v5 on v4

--- a/solution.py
+++ b/solution.py
@@ -49,8 +49,7 @@
     return (0.5 + 0.5 * t) + half * (1.0 - t * t) * (C0 + (3.0 * C1) * x2)
 
 
-def remote(src, dst, send, recv, seg=None, video=None):
-    where = {"seg": seg} if video is None else {"video": video}
+def remote(src, dst, send, recv, **where):
     return pltpu.make_async_remote_copy(
         src_ref=src,
         dst_ref=dst,
@@ -88,6 +87,7 @@
     qin,
     zst,
     zbuf,
+    zfar,
     ow,
     owall,
     heads,
@@ -112,6 +112,7 @@
     q_recv,
     o_send,
     o_recv,
+    m_recv,
     z_send,
     z_recv,
     h_send,
@@ -119,7 +120,10 @@
     a_recv,
     r_send,
     r_recv,
+    f_send,
+    f_recv,
     ring_sem,
+    pair_sem,
 ):
     me = lax.axis_index("seg")
     vid = lax.axis_index("video")
@@ -158,9 +162,11 @@
     for target in (at(x, y1, core), at(x, y2, core), at(x, y3, core), right, left, mate):
         tell(barrier, seg=target)
 
+    tell(barrier, video=across)
+
     @pl.when(is_worker)
     def _():
-        for target in (upper, lower, across):
+        for target in (upper, lower):
             tell(barrier, video=target)
 
     lane = lax.broadcasted_iota(jnp.int32, (16, 16), 1)
@@ -180,7 +186,7 @@
     lax.fori_loop(0, 8, prepare, 0)
     acc[...] = jnp.zeros_like(acc)
     arrived(wall.at[me], w_sem)
-    pl.semaphore_wait(barrier, jnp.where(is_worker, 9, 6))
+    pl.semaphore_wait(barrier, jnp.where(is_worker, 9, 7))
 
     def y_of(k):
         return jnp.where(k == 0, y, jnp.where(k == 1, y1, jnp.where(k == 2, y2, y3)))
@@ -349,7 +355,7 @@
     my_rows = pl.ds(pl.multiple_of(me * 64, 64), 64)
 
     def give_out_weight(i):
-        target = OWN + (i + me) % WORKERS
+        target = OWN + 2 * ((i + chip) % (WORKERS // 2)) + core
         remote(ow, owall.at[my_rows], o_send, o_recv, seg=target).start()
 
     def piece_place(s, t):
@@ -374,6 +380,11 @@
             target, place = piece_place(s, t + back * (3 - 2 * t))
             remote(zst.at[j, t], zbuf.at[place, slot], z_send, z_recv.at[place], seg=target).start()
 
+        def give_across(j, t):
+            target, _ = piece_place(seg_of(j), t + back * (3 - 2 * t))
+            remote(zst.at[j, t], zfar.at[slot], f_send, f_recv, seg=target, video=across).start()
+
+        tell(pair_sem, video=across)
         grads[...] = jnp.zeros_like(grads)
         row_block = lax.broadcasted_iota(jnp.int32, (ROWS, ROWS), 0) // MINI
         upto = row_block >= lax.broadcasted_iota(jnp.int32, (ROWS, ROWS), 1) // MINI
@@ -403,7 +414,7 @@
                 rows = slice(MINI * t, MINI * (t + 1))
                 c = nt(h[rows], q_weights[slot, t])
                 rho = lax.rsqrt(jnp.mean(c * c, -1, keepdims=True) + EPS)
-                zst[j, t, :, 0:HS] = p_query[slot, rows].astype(f32) + c * rho
+                zst[j, t, :, 0:HS] = (p_query[slot, rows].astype(f32) + c * rho).astype(bf16)
 
         def answer_queries(slot, keys, layer_one, grad, j):
             query_answers(slot, query_hidden(slot, keys, layer_one, grad), j, range(4))
@@ -485,13 +496,16 @@
             if not begin:
                 for t in range(4):
                     give_answer(before, t)
+            if end:
+                for t in range(4):
+                    give_across(before, t)
             return pre
 
         def send_out_weight(i, carry):
             give_out_weight(i)
             return carry
 
-        lax.fori_loop(0, WORKERS, send_out_weight, 0)
+        lax.fori_loop(0, WORKERS // 2, send_out_weight, 0)
         wait_for(0)
         pre = nn(qin[seg_of(0), 0:MINI, 0:HS], first[...])
         lay_out(0, 0)
@@ -499,7 +513,21 @@
 
         def two_segments(i, pre):
             pre = segment(2 * i + 1, pre, 1)
-            return segment(2 * i + 2, pre, 0)
+            pre = segment(2 * i + 2, pre, 0)
+
+            @pl.when(i == 1)
+            def _():
+                pl.semaphore_wait(pair_sem, 1)
+                for j in range(3):
+                    for t in range(4):
+                        give_across(j, t)
+
+            @pl.when(i == SEGS // 2 - 2)
+            def _():
+                for t in range(4):
+                    give_across(SEGS - 3, t)
+
+            return pre
 
         pre = lax.fori_loop(0, SEGS // 2 - 1, two_segments, pre)
         segment(SEGS - 1, pre, 1, end=True)
@@ -507,19 +535,20 @@
         answer_queries(1, qin[s_last, 0:ROWS, 0:HS], first[...], grads[...], SEGS - 1)
         for t in range(4):
             give_answer(SEGS - 1, t)
+            give_across(SEGS - 1, t)
 
     @pl.when(is_worker)
     def _():
         lax.fori_loop(0, 4, later_given, 0)
 
         def send_out_weight(i, carry):
-            @pl.when(OWN + (i + me) % WORKERS != me)
+            @pl.when(OWN + 2 * ((i + chip) % (WORKERS // 2)) + core != me)
             def _():
                 give_out_weight(i)
 
             return carry
 
-        lax.fori_loop(0, WORKERS, send_out_weight, 0)
+        lax.fori_loop(0, WORKERS // 2, send_out_weight, 0)
         pltpu.make_async_copy(ow, owall.at[my_rows], o_recv).start()
 
         for k in range(3):
@@ -554,12 +583,24 @@
 
             lax.fori_loop(1, 8, one, 0)
 
+        def write_heads(place, columns, answers):
+            for v in range(VIDEOS):
+                both = [answers[i].astype(f32) for i in (2 * v, 2 * v + 1, 2 * v + 4, 2 * v + 5)]
+                pair = [both[h] + both[2 + h] for h in range(2)]
+                heads[place, MINI * v : MINI * (v + 1), columns] = jnp.concatenate(pair, 1).astype(bf16)
+
+        def gather_last():
+            arrived(zbuf.at[0], z_recv.at[0])
+            write_heads(0, mine, [zbuf[0, i, :, 0:HS] for i in range(8)])
+            spread(0, mine)
+            arrived(zfar, f_recv)
+            write_heads(0, theirs, [zfar[i, :, 0:HS] for i in range(8)])
+            spread(0, theirs)
+
         def gather(n):
             place, _, _ = place_of(n)
             arrived(zbuf.at[place], z_recv.at[place])
-            for v in range(VIDEOS):
-                pair = [zbuf[place, 2 * v + h, :, 0:HS] + zbuf[place, 4 + 2 * v + h, :, 0:HS] for h in range(2)]
-                heads[place, MINI * v : MINI * (v + 1), mine] = jnp.concatenate(pair, 1).astype(bf16)
+            write_heads(place, mine, [zbuf[place, i, :, 0:HS] for i in range(8)])
             block = heads.at[place, :, mine]
             remote(block, block, h_send.at[place], a_recv.at[place], video=across).start()
             spread(place, mine)
@@ -592,21 +633,39 @@
 
             return carry
 
+        half_of_all = owall.at[pl.ds(0, 1024)]
+        arrived(half_of_all, o_recv)
+
+        def share(i, carry):
+            block = owall.at[pl.ds(pl.multiple_of((2 * i + core) * 64, 64), 64)]
+            remote(block, block, o_send, m_recv, seg=mate).start()
+            return carry
+
+        lax.fori_loop(0, 16, share, 0)
         gather(0)
         gather(1)
-        arrived(owall, o_recv)
-        lax.fori_loop(2, count, piece, 0)
+        arrived(half_of_all, m_recv)
+        lax.fori_loop(2, count - 1, piece, 0)
+        relay(count - 3)
+        finish(count - 5)
         relay(count - 2)
         finish(count - 4)
+        gather_last()
         finish(count - 3)
-        relay(count - 1)
         finish(count - 2)
         finish(count - 1)
 
         def piece_sent(n, carry):
             i = 12 * n + p
             s = jnp.where(upper_half == 0, i // 4, SEGS - 1 - i // 4)
-            arrived(heads.at[n, :, pl.ds(0, 128 * (GROUPS - 1))], h_send.at[n])
+
+            @pl.when(n == 0)
+            def _():
+                arrived(heads.at[n, :, pl.ds(0, 128 * 14)], h_send.at[n])
+
+            @pl.when(n > 0)
+            def _():
+                arrived(heads.at[n, :, pl.ds(0, 128 * 15)], h_send.at[n])
 
             @pl.when(s != me)
             def _():
@@ -615,7 +674,7 @@
             return carry
 
         lax.fori_loop(0, count, piece_sent, 0)
-        arrived(owall.at[pl.ds(0, 64 * (WORKERS - 1))], o_send)
+        arrived(owall.at[pl.ds(0, 64 * (WORKERS // 2 - 1 + 16))], o_send)
         loads[5].wait()
         loads[6].wait()
 
@@ -623,8 +682,9 @@
     def _():
         lax.fori_loop(0, 4, soon_given, 0)
         lax.fori_loop(0, 4, later_given, 0)
-        arrived(owall.at[pl.ds(0, 64 * WORKERS)], o_send)
+        arrived(owall.at[pl.ds(0, 64 * (WORKERS // 2))], o_send)
         arrived(zst, z_send)
+        arrived(zst.at[pl.ds(0, 6)], f_send)
 
     arrived(wall.at[pl.ds(0, SEGS - 1)], w_send)
 
@@ -654,8 +714,9 @@
             pltpu.VMEM((VIDEOS * ROWS, 384), f32),
             pltpu.VMEM((8, 96, 128), bf16),
             pltpu.VMEM((SEGS, 96, 128), bf16),
-            pltpu.VMEM((SEGS, 4, MINI, 128), f32),
-            pltpu.VMEM((6, 8, MINI, 128), f32),
+            pltpu.VMEM((SEGS, 4, MINI, 128), bf16),
+            pltpu.VMEM((6, 8, MINI, 128), bf16),
+            pltpu.VMEM((8, MINI, 128), bf16),
             pltpu.VMEM((64, 192), bf16),
             pltpu.VMEM((2048, 192), bf16),
             pltpu.VMEM((6, VIDEOS * MINI, 2048), bf16),
@@ -681,13 +742,17 @@
             dma,
             dma,
             dma,
+            dma,
             dma((6,)),
             dma((6,)),
             dma((6,)),
             dma((6,)),
             dma((6,)),
             dma,
+            dma,
+            dma,
             pltpu.SemaphoreType.REGULAR((4,)),
+            pltpu.SemaphoreType.REGULAR,
         ],
         compiler_params=pltpu.CompilerParams(
             collective_id=0, has_side_effects=True, vmem_limit_bytes=60 << 20

time: 102 us -> 98.2 us (0.963); the launches traced: 100 us -> 98 us
  Pallas kernels: 98.9 us -> 96.5 us
    pallas_call x1, Pallas kernels: 98.9 us -> 96.5 us  [per_device(): pl.pallas_call(kernel, out_shape=jax.ShapeDtypeStruct((VIDEOS, ROWS, 192)...]
where the time goes in v5:
time: 98.2 us; the launch traced here: 98 us
  Pallas kernels  96.5 us (98%)
  local copies, waits for them, and re-layouts  1.47 us (1%)
    pallas_call x1, Pallas kernels, per_device(): pl.pallas_call(kernel, out_shape=jax.ShapeDtypeStruct((VIDEOS, ROWS, 192)...  96.5 us

profile of v5, /device:TPU:1, one launch (start us, length us, event | category | flops | bytes accessed | tf_op | source)
XLA Modules:
  0.0 98.0 jit_solution(3924889507201458533)
XLA Ops:
  0.0 96.5 %chains.1 = bf16[2,64,192]{2,1,0:T(8,128)(2,1)} custom-call(f32[2]{0:T(128)} %rate_ref.1, s32[1,2]{1,0:T(1,128)} %bitcast.3, bf16[2,64,3072]{2,1,0:T(8,128)(2,1)} %tok_ref.1, bf16[16,3072]{1,0:T(8,128)(2,1)} %table_ref.1, bf16[3,96,128]{2,1,0:T(8,128)(2,1)} %bitcast.2, bf16[64,192]{1,0:T(8,128)(2,1)} %ow_ref.1, bf16[2,64,256]{2,1,0:T(8,128)(2,1)} %first_ref.1, ...), custom_call_target="tpu_custom_call" | custom-call | tf_op jit(solution)/shard_map/chains/pallas_call | solution.py:704
  96.5 1.5 %copy.10 = bf16[2,64,192]{2,1,0:T(8,128)(2,1)} copy(bf16[2,64,192]{2,1,0:T(8,128)(2,1)} %chains.1) | data formatting | bytes 98304

commit v6 on v5

--- a/solution.py
+++ b/solution.py
@@ -397,12 +397,14 @@
             s = seg_of(j)
             keys = qin[s, 0:ROWS, 0:HS]
             targets = jnp.concatenate([qin[s, ROWS:96, 0:HS], qin[s, ROWS:96, HS:128]], 0)
-            p_query[slot] = qin[s, 0:ROWS, HS:128]
             p_turned[slot] = keys.T
             targets = targets.astype(f32)
             p_target[slot] = targets
             for t in range(4):
                 p_across[slot, t] = targets[MINI * t : MINI * (t + 1)].T
+
+        def lay_out_queries(j, slot):
+            p_query[slot] = qin[seg_of(j), 0:ROWS, HS:128]
 
         def query_hidden(slot, keys, layer_one, grad):
             queries = p_query[slot]
@@ -435,13 +437,13 @@
                 layer_before = layer_one
                 layer_one = (layer_one.astype(f32) - eta * nn(p_turned[1 - slot], grads_before)).astype(bf16)
                 first[...] = layer_one
-            base_k = nn(keys_ahead, layer_one)
+            base_k = nn(keys_ahead[:MINI], layer_one)
             cross = -eta * nt(keys_ahead, keys)
             cross_b = cross.astype(bf16)
             layer_two = second[...].astype(f32)
             mu = jnp.mean(layer_two, 0, keepdims=True)
             centred = layer_two - mu
-            ahead = [base_k[MINI * t : MINI * (t + 1)] for t in range(4)]
+            ahead = [base_k]
             done = []
             for t in range(4):
                 rows = slice(MINI * t, MINI * (t + 1))
@@ -475,9 +477,14 @@
                     term = jnp.broadcast_to(col, (MINI, 256)) * jnp.broadcast_to(grad[i : i + 1], (MINI, 256))
                     sums[i % 2] = term if sums[i % 2] is None else sums[i % 2] + term
                 pre = sums[0] + sums[1]
+                if t == 0:
+                    rest = nn(keys_ahead[MINI:], layer_one)
+                    ahead += [rest[MINI * i : MINI * (i + 1)] for i in range(3)]
                 for r in range(t + 1, 4):
                     ahead[r] = ahead[r] + nn(cross_b[MINI * r : MINI * (r + 1), rows], grad_b)
                 q_weights[slot, t] = moved.astype(bf16)
+                if t == 3 and not end:
+                    lay_out(j + 1, 1 - slot)
                 centred = moved
                 if t == 0 and not begin:
                     h_query = query_hidden(1 - slot, keys_before, layer_before, grads_before)
@@ -492,7 +499,7 @@
             grads[...] = jnp.concatenate(done, 0)
             second[...] = (centred + mu).astype(bf16)
             if not end:
-                lay_out(j + 1, 1 - slot)
+                lay_out_queries(j + 1, 1 - slot)
             if not begin:
                 for t in range(4):
                     give_answer(before, t)
@@ -509,6 +516,7 @@
         wait_for(0)
         pre = nn(qin[seg_of(0), 0:MINI, 0:HS], first[...])
         lay_out(0, 0)
+        lay_out_queries(0, 0)
         pre = segment(0, pre, 0, begin=True)
 
         def two_segments(i, pre):

time: 98.2 us -> 95.5 us (0.973)
  Pallas kernels: 96.5 us -> 93.8 us
    pallas_call x1, Pallas kernels: 96.5 us -> 93.8 us  [per_device(): pl.pallas_call(kernel, out_shape=jax.ShapeDtypeStruct((VIDEOS, ROWS, 192)...]
where the time goes in v6:
time: 95.5 us; the launch traced here: 95.3 us
  Pallas kernels  93.8 us (98%)
  local copies, waits for them, and re-layouts  1.47 us (2%)
    pallas_call x1, Pallas kernels, per_device(): pl.pallas_call(kernel, out_shape=jax.ShapeDtypeStruct((VIDEOS, ROWS, 192)...  93.8 us

profile of v6, /device:TPU:1, one launch (start us, length us, event | category | flops | bytes accessed | tf_op | source)
XLA Modules:
  0.0 95.3 jit_solution(17972681069003204456)
XLA Ops:
  0.0 93.8 %chains.1 = bf16[2,64,192]{2,1,0:T(8,128)(2,1)} custom-call(f32[2]{0:T(128)} %rate_ref.1, s32[1,2]{1,0:T(1,128)} %bitcast.3, bf16[2,64,3072]{2,1,0:T(8,128)(2,1)} %tok_ref.1, bf16[16,3072]{1,0:T(8,128)(2,1)} %table_ref.1, bf16[3,96,128]{2,1,0:T(8,128)(2,1)} %bitcast.2, bf16[64,192]{1,0:T(8,128)(2,1)} %ow_ref.1, bf16[2,64,256]{2,1,0:T(8,128)(2,1)} %first_ref.1, ...), custom_call_target="tpu_custom_call" | custom-call | tf_op jit(solution)/shard_map/chains/pallas_call | solution.py:712
  93.8 1.5 %copy.10 = bf16[2,64,192]{2,1,0:T(8,128)(2,1)} copy(bf16[2,64,192]{2,1,0:T(8,128)(2,1)} %chains.1) | data formatting | bytes 98304

commit v7 on v6

--- a/solution.py
+++ b/solution.py
@@ -273,12 +273,16 @@
         for part in range(PARTS):
             landed(far, part)
             pass_on(far, part, mate)
-        add(far)
+        return carry
+
+    def add_rest(k, carry):
+        add(at(x + 2, y_of(k), core))
         for i in (0, 1, 3):
             other_add(at(x + i, y_of(k), 1 - core))
         return carry
 
     lax.fori_loop(0, 4, far_step, 0)
+    lax.fori_loop(0, 4, add_rest, 0)
 
     def last_step(k, carry):
         other_add(at(x + 2, y_of(k), 1 - core))

time: 95.5 us -> 96.5 us (1.010)
  Pallas kernels: 93.8 us -> 94.8 us
    pallas_call x1, Pallas kernels: 93.8 us -> 94.8 us  [per_device(): pl.pallas_call(kernel, out_shape=jax.ShapeDtypeStruct((VIDEOS, ROWS, 192)...]
where the time goes in v7:
time: 96.5 us; the launch traced here: 96.3 us
  Pallas kernels  94.8 us (98%)
  local copies, waits for them, and re-layouts  1.47 us (2%)
    pallas_call x1, Pallas kernels, per_device(): pl.pallas_call(kernel, out_shape=jax.ShapeDtypeStruct((VIDEOS, ROWS, 192)...  94.8 us

profile of v7, /device:TPU:1, one launch (start us, length us, event | category | flops | bytes accessed | tf_op | source)
XLA Modules:
  0.0 96.3 jit_solution(2205955617104713742)
XLA Ops:
  0.0 94.8 %chains.1 = bf16[2,64,192]{2,1,0:T(8,128)(2,1)} custom-call(f32[2]{0:T(128)} %rate_ref.1, s32[1,2]{1,0:T(1,128)} %bitcast.3, bf16[2,64,3072]{2,1,0:T(8,128)(2,1)} %tok_ref.1, bf16[16,3072]{1,0:T(8,128)(2,1)} %table_ref.1, bf16[3,96,128]{2,1,0:T(8,128)(2,1)} %bitcast.2, bf16[64,192]{1,0:T(8,128)(2,1)} %ow_ref.1, bf16[2,64,256]{2,1,0:T(8,128)(2,1)} %first_ref.1, ...), custom_call_target="tpu_custom_call" | custom-call | tf_op jit(solution)/shard_map/chains/pallas_call | solution.py:716
  94.8 1.5 %copy.10 = bf16[2,64,192]{2,1,0:T(8,128)(2,1)} copy(bf16[2,64,192]{2,1,0:T(8,128)(2,1)} %chains.1) | data formatting | bytes 98304
